TPU v7x, 128 devices: a whole 4x4x4 slice. The times are simulated.
128 devices in a mesh: grp: 8 (over z_lo, x), own: 16 (over y, z_hi, core).
Axes of the slice: x: 4, y: 4, z: 4 (z_hi: 2, z_lo: 2; z = z_hi * 2 + z_lo), core: 2. Of those that a mesh axis runs over, the one named last changes fastest.
Arguments:
- hidden_in: bfloat16 [16, 2048, 1024], P('own', 'grp'), may hold values from -6 to 6
- cotangent: bfloat16 [16, 2048, 1024], P('own', 'grp'), may hold values from -6 to 6
- segment_ids: int32 [16, 2048], P('own'), may hold values from 0 to 12, as said below
- live_slots: int32 [16, 2048], P('own'), may hold values from 0 to 1, as said below
- w_qkv: bfloat16 [1024, 3072], P('grp'), may hold values from -0.1875 to 0.1875
- w_out: bfloat16 [1024, 1024], P('grp'), may hold values from -0.75 to 0.75
- w_up: bfloat16 [1024, 4096], P('grp'), may hold values from -0.1875 to 0.1875
- w_down: bfloat16 [4096, 1024], P('grp'), may hold values from -0.09375 to 0.09375
- w_vec: bfloat16 [1024, 13], P('grp'), as said below
- master_qkv: float32 [1024, 3072], P('grp'), may hold values from -0.1875 to 0.1875
- master_out: float32 [1024, 1024], P('grp'), may hold values from -0.75 to 0.75
- master_up: float32 [1024, 4096], P('grp'), may hold values from -0.1875 to 0.1875
- master_down: float32 [4096, 1024], P('grp'), may hold values from -0.09375 to 0.09375
- master_vec: float32 [1024, 13], P('grp'), as said below
- first_qkv: float32 [1024, 3072], P('grp'), may hold values from -2048 to 2048
- first_out: float32 [1024, 1024], P('grp'), may hold values from -320 to 320
- first_up: float32 [1024, 4096], P('grp'), may hold values from -256 to 256
- first_down: float32 [4096, 1024], P('grp'), may hold values from -640 to 640
- first_vec: float32 [1024, 13], P('grp'), may hold values from -1024 to 1024
- second_qkv: float32 [1024, 3072], P('grp'), may hold values from 65536 to 1048576
- second_out: float32 [1024, 1024], P('grp'), may hold values from 1474.56 to 23592.96
- second_up: float32 [1024, 4096], P('grp'), may hold values from 983.04 to 16384
- second_down: float32 [4096, 1024], P('grp'), may hold values from 5898.24 to 94371.84
- second_vec: float32 [1024, 13], P('grp'), may hold values from 16384 to 262144
Outputs:
- layer_out: bfloat16 [16, 2048, 1024], P('own', 'grp')
- input_grad: float32 [16, 2048, 1024], P('own', 'grp')
- new_master_qkv: float32 [1024, 3072], P('grp')
- new_master_out: float32 [1024, 1024], P('grp')
- new_master_up: float32 [1024, 4096], P('grp')
- new_master_down: float32 [4096, 1024], P('grp')
- new_master_vec: float32 [1024, 13], P('grp')
- new_first_qkv: float32 [1024, 3072], P('grp')
- new_first_out: float32 [1024, 1024], P('grp')
- new_first_up: float32 [1024, 4096], P('grp')
- new_first_down: float32 [4096, 1024], P('grp')
- new_first_vec: float32 [1024, 13], P('grp')
- new_second_qkv: float32 [1024, 3072], P('grp')
- new_second_out: float32 [1024, 1024], P('grp')
- new_second_up: float32 [1024, 4096], P('grp')
- new_second_down: float32 [4096, 1024], P('grp')
- new_second_vec: float32 [1024, 13], P('grp')
- copy_qkv: bfloat16 [1024, 3072], P('grp')
- copy_out: bfloat16 [1024, 1024], P('grp')
- copy_up: bfloat16 [1024, 4096], P('grp')
- copy_down: bfloat16 [4096, 1024], P('grp')
- copy_vec: bfloat16 [1024, 13], P('grp')
Inputs may be any that keep to these rules, and one draw needn't show every extreme that they name: `segment_ids`: each row holds one tree in depth-first order: trunk (segment 0), then for branch b = 1 to 4 the branch (segment b) followed by its two leaves (segments 2 b + 3 and 2 b + 4); a branch has 64 to 128 slots, a leaf 64 // 2 to 64; the trunk fills the row but for fewer than 32 slots after the last leaf, which carry segment 12. `live_slots`: 1 exactly on the slots of the tree, 0 on the slots after it. `w_vec`: columns 0 and 2 lie in 0.6 to 1.4, the others in -0.2 to 0.2. `master_vec`: columns 0 and 2 lie in 0.6 to 1.4, the others in -0.2 to 0.2.
All inputs are finite; a program needn't handle non-finite values.
Results may differ from a plain program's by a relative error of at most 0.003.
The roundings to bfloat16 on the way count: a program that leaves them out, or rounds other values in their place, can miss the bound.
Values may be sent and summed in bfloat16 or wider, within the bound.
No kernel may reach another device: no remote copies, remote signals or barrier semaphores. Data moves between devices by JAX's collectives and lax.ppermute only.
A program may use at most 320 MiB of HBM per device.

v0:
```python
from functools import partial
import math

import jax
import jax.numpy as jnp
from jax import lax
from jax.sharding import PartitionSpec as P

HEADS = 16
HD = 64
ROT = 16
STEP = 5


norm_eps = 1e-05
adam_beta = 0.5
adam_eps = 1e-08
weight_decay = 0.01
learn_rates = (0.02, 0.1, 0.02, 0.01, 0.2)
head_group = 4


def normalize(inputs):
    center = inputs - jnp.mean(inputs, axis=-1, keepdims=True)
    inverse = lax.rsqrt(jnp.mean(center * center, axis=-1, keepdims=True) + norm_eps)
    return (center * inverse, inverse)


def norm_back(grad_norm, normed, inverse):
    mean_one = jnp.mean(grad_norm, axis=-1, keepdims=True)
    mean_two = jnp.mean(grad_norm * normed, axis=-1, keepdims=True)
    return inverse * (grad_norm - mean_one - normed * mean_two)


def rotary(tensor, cos_table, sin_table, direction):
    half_dim = cos_table.shape[-1]
    front_half = tensor[..., :half_dim]
    back_half = tensor[..., half_dim : 2 * half_dim]
    cos_part = cos_table[:, None, :]
    sin_part = direction * sin_table[:, None, :]
    return jnp.concatenate(
        [
            front_half * cos_part - back_half * sin_part,
            back_half * cos_part + front_half * sin_part,
            tensor[..., 2 * half_dim :],
        ],
        axis=-1,
    )


def branch_of(segment):
    return jnp.where(segment >= 5, 1 + (segment - 5) // 2, segment)


def path_mask(query_seg, key_seg, query_pos, key_pos, key_live):
    same_seg = key_seg[None, :] == query_seg[:, None]
    trunk_key = key_seg[None, :] == 0
    parent_key = (query_seg[:, None] >= 5) & (key_seg[None, :] == branch_of(query_seg)[:, None])
    causal = key_pos[None, :] <= query_pos[:, None]
    return (same_seg | trunk_key | parent_key) & causal & (key_live[None, :] == 1)


def scores_of(queries, key_all, allowed, scale):
    scores = (
        jnp.einsum("qhd,khd->hqk", queries, key_all, preferred_element_type=jnp.float32) * scale
    )
    return jnp.where(allowed[None], scores, -1e30)


def attend_forward(queries, key_all, value_all, allowed, scale):
    outputs = []
    log_sums = []
    for head_start in range(0, queries.shape[1], head_group):
        head_range = slice(head_start, head_start + head_group)
        scores = scores_of(queries[:, head_range], key_all[:, head_range], allowed, scale)
        row_max = jnp.max(scores, axis=-1, keepdims=True)
        exp_scores = jnp.exp(scores - row_max)
        exp_total = jnp.sum(exp_scores, axis=-1, keepdims=True)
        attn_probs = (exp_scores / exp_total).astype(jnp.bfloat16)
        outputs.append(
            jnp.einsum(
                "hqk,khd->qhd",
                attn_probs,
                value_all[:, head_range],
                preferred_element_type=jnp.float32,
            )
        )
        log_sums.append((row_max + jnp.log(exp_total))[..., 0])
    return (jnp.concatenate(outputs, axis=1), jnp.concatenate(log_sums, axis=0))


def attend_backward(queries, key_all, value_all, allowed, log_sums, grad_attn, scale):
    grad_query = []
    grad_key = []
    grad_value = []
    for head_start in range(0, queries.shape[1], head_group):
        head_range = slice(head_start, head_start + head_group)
        scores = scores_of(queries[:, head_range], key_all[:, head_range], allowed, scale)
        attn_probs = jnp.exp(scores - log_sums[head_range][..., None])
        grad_probs = jnp.einsum(
            "qhd,khd->hqk",
            grad_attn[:, head_range],
            value_all[:, head_range],
            preferred_element_type=jnp.float32,
        )
        row_delta = jnp.sum(grad_probs * attn_probs, axis=-1, keepdims=True)
        grad_scores = (attn_probs * (grad_probs - row_delta)).astype(jnp.bfloat16)
        grad_query.append(
            jnp.einsum(
                "hqk,khd->qhd",
                grad_scores,
                key_all[:, head_range],
                preferred_element_type=jnp.float32,
            )
            * scale
        )
        grad_key.append(
            jnp.einsum(
                "hqk,qhd->khd",
                grad_scores,
                queries[:, head_range],
                preferred_element_type=jnp.float32,
            )
            * scale
        )
        grad_value.append(
            jnp.einsum(
                "hqk,qhd->khd",
                attn_probs.astype(jnp.bfloat16),
                grad_attn[:, head_range],
                preferred_element_type=jnp.float32,
            )
        )
    return (
        jnp.concatenate(grad_query, axis=1),
        jnp.concatenate(grad_key, axis=1),
        jnp.concatenate(grad_value, axis=1),
    )


def product_term(left_side, right_side, first_row, row_span):
    sliced = lax.dynamic_slice_in_dim(left_side, first_row, row_span, 1)
    return jnp.einsum("tr,tc->rc", sliced, right_side, preferred_element_type=jnp.float32)


def adamw_apply(operands, learn_rate):
    master, first_mom, second_mom, gradient = operands
    first_new = adam_beta * first_mom + (1.0 - adam_beta) * gradient
    second_new = adam_beta * second_mom + (1.0 - adam_beta) * gradient * gradient
    correction = 1.0 - adam_beta**STEP
    adam_step = first_new / correction / (jnp.sqrt(second_new / correction) + adam_eps)
    master_new = master - learn_rate * (adam_step + weight_decay * master)
    return (master_new, first_new, second_new)


def body(
    hidden_in,
    cotangent,
    segment_ids,
    live_slots,
    w_qkv,
    w_out,
    w_up,
    w_down,
    w_vec,
    master_qkv,
    master_out,
    master_up,
    master_down,
    master_vec,
    first_qkv,
    first_out,
    first_up,
    first_down,
    first_vec,
    second_qkv,
    second_out,
    second_up,
    second_down,
    second_vec,
):
    group_size = lax.axis_size("grp")
    group_pos = lax.axis_index("grp")
    whole = (
        lax.all_gather(w_qkv, "grp", axis=0, tiled=True),
        lax.all_gather(w_out, "grp", axis=0, tiled=True),
        lax.all_gather(w_up, "grp", axis=0, tiled=True),
        lax.all_gather(w_down, "grp", axis=0, tiled=True),
        lax.all_gather(w_vec, "grp", axis=0, tiled=True),
    )
    full_qkv, full_out, full_up, full_down, full_vec = whole
    vectors = full_vec.astype(jnp.float32)
    row_count, local_len, width = hidden_in.shape
    seq_len = local_len * group_size
    tok_count = row_count * local_len
    scale = 1.0 / math.sqrt(HD)
    inputs = hidden_in.reshape(tok_count, width).astype(jnp.float32)
    back_out = cotangent.reshape(tok_count, width)
    back_wide = back_out.astype(jnp.float32)
    normed, inverse = normalize(inputs)
    norm_one = (normed * vectors[:, 0] + vectors[:, 1]).astype(jnp.bfloat16)
    norm_two = (normed * vectors[:, 2] + vectors[:, 3]).astype(jnp.bfloat16)
    bias_qkv = jnp.concatenate([vectors[:, 4], vectors[:, 5], vectors[:, 6]])
    bias_up = vectors[:, 9:].T.reshape(-1)
    projected = jnp.dot(norm_one, full_qkv, preferred_element_type=jnp.float32) + bias_qkv
    query_pos = group_pos * local_len + jnp.arange(local_len)
    inv_freq = 10000.0 ** (-jnp.arange(0, ROT, 2).astype(jnp.float32) / ROT)
    angles = query_pos.astype(jnp.float32)[:, None] * inv_freq[None, :]
    cos_table = jnp.cos(angles)
    sin_table = jnp.sin(angles)
    split_qkv = projected.reshape(row_count, local_len, 3, HEADS, HD)
    queries = rotary(split_qkv[:, :, 0], cos_table, sin_table, 1.0).astype(jnp.bfloat16)
    key_local = (
        rotary(split_qkv[:, :, 1], cos_table, sin_table, 1.0)
        .astype(jnp.bfloat16)
        .reshape(row_count, local_len, width)
    )
    value_local = split_qkv[:, :, 2].astype(jnp.bfloat16).reshape(row_count, local_len, width)
    key_rows, value_rows = (
        lax.all_gather(key_local, "grp", axis=1, tiled=True),
        lax.all_gather(value_local, "grp", axis=1, tiled=True),
    )
    key_pos = jnp.arange(seq_len)
    row_index = 0
    query_seg = lax.dynamic_slice_in_dim(
        segment_ids[row_index], group_pos * local_len, local_len, 0
    )
    masks = [
        path_mask(query_seg, segment_ids[row_index], query_pos, key_pos, live_slots[row_index])
    ]
    row_index = 0
    attn_row, log_sums = attend_forward(
        queries[row_index],
        key_rows[row_index].reshape(seq_len, HEADS, HD),
        value_rows[row_index].reshape(seq_len, HEADS, HD),
        masks[row_index],
        scale,
    )
    attn_parts = attn_row.reshape(local_len, width)
    sum_parts = [log_sums]
    attn_low = attn_parts.astype(jnp.bfloat16)
    out_attn = jnp.dot(attn_low, full_out, preferred_element_type=jnp.float32) + vectors[:, 7]
    pre_act = jnp.dot(norm_two, full_up, preferred_element_type=jnp.float32) + bias_up
    act_wide, gelu_pull = jax.vjp(partial(jax.nn.gelu, approximate=False), pre_act)
    act_low = act_wide.astype(jnp.bfloat16)
    out_mlp = jnp.dot(act_low, full_down, preferred_element_type=jnp.float32) + vectors[:, 8]
    layer_out = (
        (inputs + out_attn + out_mlp).astype(jnp.bfloat16).reshape(row_count, local_len, width)
    )
    grad_attn = jnp.einsum(
        "tc,rc->tr", back_out, full_out, preferred_element_type=jnp.float32
    ).astype(jnp.bfloat16)
    grad_act = jnp.einsum("tc,rc->tr", back_out, full_down, preferred_element_type=jnp.float32)
    grad_pre = gelu_pull(grad_act)[0].astype(jnp.bfloat16)
    key_use, value_use = (key_rows, value_rows)
    grad_attn_rows = grad_attn.reshape(row_count, local_len, HEADS, HD)
    row_index = 0
    grad_query, grad_key, grad_value = attend_backward(
        queries[row_index],
        key_use[row_index].reshape(seq_len, HEADS, HD),
        value_use[row_index].reshape(seq_len, HEADS, HD),
        masks[row_index],
        sum_parts[row_index],
        grad_attn_rows[row_index],
        scale,
    )
    query_grads = [grad_query]
    key_grads = [grad_key.reshape(seq_len, width)]
    value_grads = [grad_value.reshape(seq_len, width)]
    key_sum, value_sum = (
        lax.psum_scatter(jnp.stack(key_grads, axis=0), "grp", scatter_dimension=1, tiled=True),
        lax.psum_scatter(jnp.stack(value_grads, axis=0), "grp", scatter_dimension=1, tiled=True),
    )
    query_back = rotary(jnp.stack(query_grads, axis=0), cos_table, sin_table, -1.0)
    key_back = rotary(key_sum.reshape(row_count, local_len, HEADS, HD), cos_table, sin_table, -1.0)
    value_back = value_sum.reshape(row_count, local_len, HEADS, HD)
    grad_qkv = (
        jnp.stack([query_back, key_back, value_back], axis=2)
        .reshape(tok_count, 3 * width)
        .astype(jnp.bfloat16)
    )
    grad_one = jnp.einsum("tc,rc->tr", grad_qkv, full_qkv, preferred_element_type=jnp.float32)
    grad_two = jnp.einsum("tc,rc->tr", grad_pre, full_up, preferred_element_type=jnp.float32)
    grad_normed = grad_one * vectors[:, 0] + grad_two * vectors[:, 2]
    input_grad = (back_wide + norm_back(grad_normed, normed, inverse)).reshape(
        row_count, local_len, width
    )
    qkv_sums = jnp.sum(grad_qkv.astype(jnp.float32), axis=0)
    out_sum = jnp.sum(back_wide, axis=0)
    up_sum = jnp.sum(grad_pre.astype(jnp.float32), axis=0)
    columns = [
        jnp.sum(grad_one * normed, axis=0),
        jnp.sum(grad_one, axis=0),
        jnp.sum(grad_two * normed, axis=0),
        jnp.sum(grad_two, axis=0),
        qkv_sums[:width],
        qkv_sums[width : 2 * width],
        qkv_sums[2 * width :],
        out_sum,
        out_sum,
    ]
    vec_grad = jnp.concatenate([jnp.stack(columns, axis=1), up_sum.reshape(-1, width).T], axis=1)

    def slice_term(first_row, row_span):
        return vec_grad

    term_list = (
        partial(product_term, norm_one, grad_qkv),
        partial(product_term, attn_low, back_out),
        partial(product_term, norm_two, grad_pre),
        partial(product_term, act_low, back_out),
        slice_term,
    )
    shard_lens = (w_qkv.shape[0], w_out.shape[0], w_up.shape[0], w_down.shape[0], w_vec.shape[0])
    reduced = tuple(
        (
            lax.psum_scatter(
                term_fn(jnp.int32(0), lax.axis_size("grp") * shard_len),
                "grp",
                scatter_dimension=0,
                tiled=True,
            )
            for term_fn, shard_len in zip(term_list, shard_lens)
        )
    )
    summed = lax.psum(reduced, "own")
    masters = (master_qkv, master_out, master_up, master_down, master_vec)
    firsts = (first_qkv, first_out, first_up, first_down, first_vec)
    seconds = (second_qkv, second_out, second_up, second_down, second_vec)
    results = []
    for mat_index in range(5):
        operands = (masters[mat_index], firsts[mat_index], seconds[mat_index], summed[mat_index])
        results.append(adamw_apply(operands, learn_rates[mat_index]))
    return (
        layer_out,
        input_grad,
        results[0][0],
        results[1][0],
        results[2][0],
        results[3][0],
        results[4][0],
        results[0][1],
        results[1][1],
        results[2][1],
        results[3][1],
        results[4][1],
        results[0][2],
        results[1][2],
        results[2][2],
        results[3][2],
        results[4][2],
        results[0][0].astype(jnp.bfloat16),
        results[1][0].astype(jnp.bfloat16),
        results[2][0].astype(jnp.bfloat16),
        results[3][0].astype(jnp.bfloat16),
        results[4][0].astype(jnp.bfloat16),
    )


def solution(mesh):
    return jax.shard_map(
        body,
        mesh=mesh,
        in_specs=(
            P("own", "grp", None),
            P("own", "grp", None),
            P("own", None),
            P("own", None),
            P("grp", None),
            P("grp", None),
            P("grp", None),
            P("grp", None),
            P("grp", None),
            P("grp", None),
            P("grp", None),
            P("grp", None),
            P("grp", None),
            P("grp", None),
            P("grp", None),
            P("grp", None),
            P("grp", None),
            P("grp", None),
            P("grp", None),
            P("grp", None),
            P("grp", None),
            P("grp", None),
            P("grp", None),
            P("grp", None),
        ),
        out_specs=(
            P("own", "grp", None),
            P("own", "grp", None),
            P("grp", None),
            P("grp", None),
            P("grp", None),
            P("grp", None),
            P("grp", None),
            P("grp", None),
            P("grp", None),
            P("grp", None),
            P("grp", None),
            P("grp", None),
            P("grp", None),
            P("grp", None),
            P("grp", None),
            P("grp", None),
            P("grp", None),
            P("grp", None),
            P("grp", None),
            P("grp", None),
            P("grp", None),
            P("grp", None),
        ),
        check_vma=False,
    )
```

profile of v0, /device:TPU:1, one launch (start us, length us, event | category | flops | bytes accessed | tf_op | source)
XLA Modules:
  0.0 1398.0 jit_solution(2951438879875286658)
XLA Ops:
  8.7 21.7 %all_gather.21 = bf16[1024,13]{0,1:T(8,128)(2,1)S(1)} all-gather(bf16[128,13]{0,1:T(8,128)(2,1)} %param.32), channel_id=1, replica_groups=mesh['grp'=8,'own'=16] {'grp'}, dimensions={0}, use_global_device_ids=true | all-gather | bytes 29952 | tf_op jit(solution)/shard_map/all_gather | solution.py:189
  35.0 50.5 %all-gather.7.cloned.1.call-done = bf16[1024,3072]{1,0:T(8,128)(2,1)} async-done(((bf16[128,3072]{1,0:T(8,128)(2,1)}), bf16[1024,3072]{1,0:T(8,128)(2,1)}) %all-gather.7.cloned.1.call-update) | async-done | bytes 6291472 | tf_op jit(solution)/shard_map/all_gather | solution.py:185
  85.5 6.5 convolution_add_fusion.1
  100.2 22.2 %all-gather.13.cloned.1.call-done = bf16[1024,1024]{1,0:T(8,128)(2,1)} async-done(((bf16[128,1024]{1,0:T(8,128)(2,1)}), bf16[1024,1024]{1,0:T(8,128)(2,1)}) %all-gather.13.cloned.1.call-update) | async-done | bytes 2097168 | tf_op jit(solution)/shard_map/all_gather | solution.py:186
  126.3 60.6 %all-gather.11.cloned.1.call-done = bf16[1,2048,1024]{1,2,0:T(8,128)(2,1)} async-done(((bf16[1,256,1024]{1,2,0:T(8,128)(2,1)}), bf16[1,2048,1024]{1,2,0:T(8,128)(2,1)}) %all-gather.11.cloned.1.call-update) | async-done | bytes 4194320 | tf_op jit(solution)/shard_map/all_gather | solution.py:220
  186.9 3.2 fusion.145
  191.5 2.9 copy-done
  212.0 38.1 %all-gather.9.cloned.1.call-done = bf16[1,2048,1024]{1,2,0:T(8,128)(2,1)} async-done(((bf16[1,256,1024]{1,2,0:T(8,128)(2,1)}), bf16[1,2048,1024]{1,2,0:T(8,128)(2,1)}) %all-gather.9.cloned.1.call-update) | async-done | bytes 4194320 | tf_op jit(solution)/shard_map/all_gather | solution.py:221
  250.0 5.5 multiply_reduce_fusion
  256.3 3.3 multiply_convert_fusion
  259.5 3.0 fusion.42
  262.6 4.0 multiply_reduce_fusion.1
  266.6 3.3 multiply_convert_fusion.1
  269.9 4.4 fusion.43
  274.3 3.9 multiply_reduce_fusion.3
  278.2 3.4 multiply_convert_fusion.3
  281.6 3.1 fusion.45
  284.8 3.8 multiply_reduce_fusion.2
  293.6 3.8 pad_maximum_fusion
  297.5 5.0 fusion.39
  302.5 5.0 fusion.36
  311.5 3.6 pad_maximum_fusion.1
  315.4 5.6 fusion.68
  321.0 5.3 fusion.69
  334.2 12.1 all-gather.15.cloned.1.call-done
  346.4 16.0 %multiply_convert_fusion.4 = (bf16[256,4096]{1,0:T(8,128)(2,1)}, f32[256,4096]{1,0:T(8,128)}, f32[256,4096]{1,0:T(8,128)}) fusion(f32[4096]{0:T(1024)S(1)} %bitcast.268, bf16[1024,4096]{1,0:T(8,128)(2,1)} %all-gather.15.cloned.1.call-done, bf16[1,256,1024]{2,1,0:T(8,128)(2,1)S(1)} %copy-done.6, f32[1024]{0:T(1024)S(1)} %bitcast.256, ...), kind=kOutput, calls=%fused_computation.47 | convolution fusion | flops 2218262528 | bytes 19425280 | tf_op jit(solution)/shard_map/dot_general | solution.py:243
  362.4 76.1 %all-gather.17.cloned.1.call-done = bf16[4096,1024]{1,0:T(8,128)(2,1)} async-done(((bf16[512,1024]{1,0:T(8,128)(2,1)}), bf16[4096,1024]{1,0:T(8,128)(2,1)}) %all-gather.17.cloned.1.call-update) | async-done | bytes 8388624 | tf_op jit(solution)/shard_map/all_gather | solution.py:188
  438.6 11.4 convert_reduce_fusion
  451.3 8.3 fusion.126
  459.9 9.7 fusion.104
  469.7 4.1 fusion.64
  481.0 51.5 %reduce-scatter.8.cloned.1.call-done = f32[1,256,1024]{1,2,0:T(8,128)} async-done(((f32[1,2048,1024]{1,2,0:T(8,128)}), f32[1,256,1024]{1,2,0:T(8,128)}) %reduce-scatter.8.cloned.1.call-update) | async-done | bytes 1048592 | tf_op jit(solution)/shard_map/reduce_scatter | solution.py:271
  536.4 90.0 %reduce-scatter.10.cloned.1.call-done = f32[1,256,1024]{1,2,0:T(8,128)} async-done(((f32[1,2048,1024]{1,2,0:T(8,128)}), f32[1,256,1024]{1,2,0:T(8,128)}) %reduce-scatter.10.cloned.1.call-update) | async-done | bytes 1048592 | tf_op jit(solution)/shard_map/reduce_scatter | solution.py:272
  628.4 6.6 fusion.101
  635.5 5.1 fusion.149
  640.7 6.3 fusion.129
  649.7 31.0 %reduce-scatter.14.cloned.1.call-done = f32[128,1024]{1,0:T(8,128)} async-done(((f32[1024,1024]{1,0:T(8,128)}), f32[128,1024]{1,0:T(8,128)}) %reduce-scatter.14.cloned.1.call-update) | async-done | bytes 524304 | tf_op jit(solution)/shard_map/reduce_scatter | solution.py:317
  680.7 172.4 %reduce-scatter.16.cloned.1.call-done = f32[128,4096]{1,0:T(8,128)} async-done(((f32[1024,4096]{1,0:T(8,128)}), f32[128,4096]{1,0:T(8,128)}) %reduce-scatter.16.cloned.1.call-update) | async-done | bytes 2097168 | tf_op jit(solution)/shard_map/reduce_scatter | solution.py:317
  853.1 172.6 %reduce-scatter.18.cloned.1.call-done = f32[512,1024]{1,0:T(8,128)} async-done(((f32[4096,1024]{1,0:T(8,128)}), f32[512,1024]{1,0:T(8,128)}) %reduce-scatter.18.cloned.1.call-update) | async-done | bytes 2097168 | tf_op jit(solution)/shard_map/reduce_scatter | solution.py:317
  1025.7 133.4 %reduce-scatter.12.cloned.1.call-done = f32[128,3072]{1,0:T(8,128)} async-done(((f32[1024,3072]{1,0:T(8,128)}), f32[128,3072]{1,0:T(8,128)}) %reduce-scatter.12.cloned.1.call-update) | async-done | bytes 1572880 | tf_op jit(solution)/shard_map/reduce_scatter | solution.py:317
  1159.2 5.9 convolution_add_fusion.3
  1166.7 25.6 %reduce-scatter.20.cloned.1.call-done = f32[128,13]{0,1:T(8,128)} async-done(((f32[1024,13]{0,1:T(8,128)}), f32[128,13]{0,1:T(8,128)}) %reduce-scatter.20.cloned.1.call-update) | async-done | bytes 6672 | tf_op jit(solution)/shard_map/reduce_scatter | solution.py:317
  1192.2 39.6 %psum.39 = f32[128,13]{0,1:T(8,128)S(1)} all-reduce(f32[128,13]{0,1:T(8,128)} %reduce-scatter.20.cloned.1.call-done), channel_id=1, replica_groups=mesh['grp'=8,'own'=16] {'own'}, use_global_device_ids=true, to_apply=%region_34.35 | all-reduce | flops 1664 | bytes 13312 | tf_op jit(solution)/shard_map/psum | solution.py:326
  1232.5 139.2 %all-reduce.3.cloned.1.call-done = (f32[128,3072]{1,0:T(8,128)}, f32[128,1024]{1,0:T(8,128)}, f32[128,4096]{1,0:T(8,128)}, f32[512,1024]{1,0:T(8,128)}) async-done(((f32[128,3072]{1,0:T(8,128)}, f32[128,1024]{1,0:T(8,128)}, f32[128,4096]{1,0:T(8,128)}, f32[512,1024]{1,0:T(8,128)}), (f32[128,3072]{1,0:T(8,128)}, f32[128,1024]{1,0:T(8,128)}, f32[128,4096]{1,0:T(8,128)}, ...) | async-done | bytes 6291472 | tf_op jit(solution)/shard_map/psum | solution.py:326
  1371.7 3.0 fusion.138
  1374.7 5.3 fusion.140
  1380.9 4.5 fusion.136
  1386.9 4.2 fusion.134
  (237 shorter events, 77.2 us)
Async XLA Ops:
  7.2 78.3 %all-gather.7.cloned.1.call-start = ((), (), s32[]{:S(2)}) async-start(), calls=%async_computation.7 | async-start | bytes 7077888 | tf_op jit(solution)/shard_map/all_gather | solution.py:185
  7.9 114.5 %all-gather.13.cloned.1.call-start = ((), (), s32[]{:S(2)}) async-start(), calls=%async_computation.10 | async-start | bytes 2359296 | tf_op jit(solution)/shard_map/all_gather | solution.py:186
  8.7 178.2 %all-gather.11.cloned.1.call-start = ((), (), s32[]{:S(2)}) async-start(), calls=%async_computation.9 | async-start | bytes 4718592 | tf_op jit(solution)/shard_map/all_gather | solution.py:220
  31.7 53.8 %copy-start.34 = (f32[1024,1]{0,1:T(1,128)}, f32[1024,1]{0,1:T(1,128)S(1)}, u32[]{:S(2)}) copy-start(f32[1024,1]{0,1:T(1,128)S(1)} %get-tuple-element.75) | copy-start | bytes 12292
  31.7 53.8 %copy-start.36 = (f32[1024,1]{0,1:T(1,128)}, f32[1024,1]{0,1:T(1,128)S(1)}, u32[]{:S(2)}) copy-start(f32[1024,1]{0,1:T(1,128)S(1)} %get-tuple-element.76) | copy-start | bytes 12292
  32.9 52.6 %copy-start.40 = (f32[256]{0:T(256)}, f32[256]{0:T(256)S(1)}, u32[]{:S(2)}) copy-start(f32[256]{0:T(256)S(1)} %broadcast_multiply_fusion.3) | copy-start | bytes 3076
  34.3 51.3 %copy-start.42 = (f32[256]{0:T(256)}, f32[256]{0:T(256)S(1)}, u32[]{:S(2)}) copy-start(f32[256]{0:T(256)S(1)} %add_rsqrt_fusion) | copy-start | bytes 3076
  35.0 59.7 %copy-start.38 = (f32[256,8]{0,1:T(8,128)}, f32[256,8]{0,1:T(8,128)S(1)}, u32[]{:S(2)}) copy-start(f32[256,8]{0,1:T(8,128)S(1)} %get-tuple-element.92) | copy-start | bytes 24580
  96.5 153.6 %all-gather.9.cloned.1.call-start = ((), (), s32[]{:S(2)}) async-start(), calls=%async_computation.8 | async-start | bytes 4718592 | tf_op jit(solution)/shard_map/all_gather | solution.py:221
  97.4 248.9 %all-gather.15.cloned.1.call-start = ((), (), s32[]{:S(2)}) async-start(), calls=%async_computation.11 | async-start | bytes 9437184 | tf_op jit(solution)/shard_map/all_gather | solution.py:187
  98.0 340.5 %all-gather.17.cloned.1.call-start = ((), (), s32[]{:S(2)}) async-start(), calls=%async_computation.12 | async-start | bytes 9437184 | tf_op jit(solution)/shard_map/all_gather | solution.py:188
  98.6 433.9 %reduce-scatter.8.cloned.1.call-start = ((), (), s32[]{:S(2)}) async-start(), calls=%async_computation.13 | async-start | bytes 9437184 | tf_op jit(solution)/shard_map/reduce_scatter | solution.py:271
  250.0 6.2 slice-start.1
  250.0 12.5 slice-start.2
  256.3 6.3 slice-start.3
  262.6 11.7 slice-start.10
  266.6 7.7 slice-start.11
  274.3 10.4 slice-start.4
  278.2 6.5 slice-start.5
  290.5 6.9 copy-start.9
  297.4 329.0 %reduce-scatter.10.cloned.1.call-start = ((), (), s32[]{:S(2)}) async-start(), calls=%async_computation.14 | async-start | bytes 9437184 | tf_op jit(solution)/shard_map/reduce_scatter | solution.py:272
  297.5 10.0 slice-start.6
  302.5 6.5 slice-start.12
  315.1 365.5 %reduce-scatter.14.cloned.1.call-start = ((), (), s32[]{:S(2)}) async-start(), calls=%async_computation.16 | async-start | bytes 4718592 | tf_op jit(solution)/shard_map/reduce_scatter | solution.py:317
  315.4 10.9 slice-start.8
  321.0 7.1 slice-start.14
  333.4 12.9 copy-start.6
  333.4 12.9 copy-start.32
  333.4 12.9 copy-start.33
  333.4 12.9 copy-start.41
  333.4 12.9 copy-start.43
  333.5 519.7 %reduce-scatter.16.cloned.1.call-start = ((), (), s32[]{:S(2)}) async-start(), calls=%async_computation.17 | async-start | bytes 18874368 | tf_op jit(solution)/shard_map/reduce_scatter | solution.py:317
  459.7 566.1 %reduce-scatter.18.cloned.1.call-start = ((), (), s32[]{:S(2)}) async-start(), calls=%async_computation.18 | async-start | bytes 18874368 | tf_op jit(solution)/shard_map/reduce_scatter | solution.py:317
  469.7 689.4 %reduce-scatter.12.cloned.1.call-start = ((), (), s32[]{:S(2)}) async-start(), calls=%async_computation.15 | async-start | bytes 14155776 | tf_op jit(solution)/shard_map/reduce_scatter | solution.py:317
  479.4 54.2 %copy-start.39 = (f32[256,8]{0,1:T(8,128)S(1)}, f32[256,8]{0,1:T(8,128)}, u32[]{:S(2)}) copy-start(f32[256,8]{0,1:T(8,128)} %copy-done.38) | copy-start | bytes 24580
  479.4 54.3 %copy-start.46 = (f32[256,8]{0,1:T(8,128)S(1)}, f32[256,8]{0,1:T(8,128)}, u32[]{:S(2)}) copy-start(f32[256,8]{0,1:T(8,128)} %get-tuple-element.90) | copy-start | bytes 24580
  480.9 147.5 %copy-start.35 = (f32[1024,1]{0,1:T(1,128)S(1)}, f32[1024,1]{0,1:T(1,128)}, u32[]{:S(2)}) copy-start(f32[1024,1]{0,1:T(1,128)} %copy-done.34) | copy-start | bytes 12292
  480.9 147.5 %copy-start.37 = (f32[1024,1]{0,1:T(1,128)S(1)}, f32[1024,1]{0,1:T(1,128)}, u32[]{:S(2)}) copy-start(f32[1024,1]{0,1:T(1,128)} %copy-done.36) | copy-start | bytes 12292
  635.0 557.2 %reduce-scatter.20.cloned.1.call-start = ((), (), s32[]{:S(2)}) async-start(), calls=%async_computation.19 | async-start | bytes 73728 | tf_op jit(solution)/shard_map/reduce_scatter | solution.py:317
  646.9 512.2 %copy-start.51 = (f32[1024,1]{0,1:T(1,128)S(1)}, f32[1024,1]{0,1:T(1,128)}, u32[]{:S(2)}) copy-start(f32[1024,1]{0,1:T(1,128)} %get-tuple-element.80) | copy-start | bytes 12292
  648.4 510.8 %copy-start.20 = (bf16[256,4096]{1,0:T(8,128)(2,1)S(1)}, bf16[256,4096]{1,0:T(8,128)(2,1)}, u32[]{:S(2)}) copy-start(bf16[256,4096]{1,0:T(8,128)(2,1)} %get-tuple-element.55) | copy-start | bytes 6291460
  649.7 722.0 %all-reduce.3.cloned.1.call-start = ((), (), s32[]{:S(2)}) async-start(), calls=%async_computation.20 | async-start | bytes 12582912 | tf_op jit(solution)/shard_map/psum | solution.py:326
  1165.0 66.9 %copy-start.47 = (f32[128,13]{0,1:T(8,128)S(1)}, f32[128,13]{0,1:T(8,128)}, u32[]{:S(2)}) copy-start(f32[128,13]{0,1:T(8,128)} %param.37) | copy-start | bytes 19972
  1165.0 66.9 %copy-start.48 = (f32[128,13]{0,1:T(8,128)S(1)}, f32[128,13]{0,1:T(8,128)}, u32[]{:S(2)}) copy-start(f32[128,13]{0,1:T(8,128)} %param.42) | copy-start | bytes 19972
  1165.0 66.8 %copy-start.49 = (f32[128,13]{0,1:T(8,128)S(1)}, f32[128,13]{0,1:T(8,128)}, u32[]{:S(2)}) copy-start(f32[128,13]{0,1:T(8,128)} %param.47) | copy-start | bytes 19972
  1165.0 206.6 %copy-start.29 = (f32[128,1024]{1,0:T(8,128)S(1)}, f32[128,1024]{1,0:T(8,128)}, u32[]{:S(2)}) copy-start(f32[128,1024]{1,0:T(8,128)} %param.34) | copy-start | bytes 1572868
  1165.1 209.6 %copy-start.27 = (f32[128,3072]{1,0:T(8,128)S(1)}, f32[128,3072]{1,0:T(8,128)}, u32[]{:S(2)}) copy-start(f32[128,3072]{1,0:T(8,128)} %param.33) | copy-start | bytes 4718596
  1374.7 6.2 copy-start.22
  (34 other events, 133.3 us)
Sparse Core Ops, SparseCore 0:
  9.7 75.7 all-gather.6
  87.1 35.2 all-gather.12
  124.6 62.2 all-gather.10
  188.9 61.0 all-gather.8
  251.5 94.7 all-gather.14
  347.8 90.6 all-gather.16
  440.9 91.4 reduce-scatter.7
  534.9 91.4 reduce-scatter.9
  628.8 51.8 reduce-scatter.13
  683.0 170.0 reduce-scatter.15
  855.6 170.0 reduce-scatter.17
  1028.0 131.0 reduce-scatter.11
  1162.0 30.1 reduce-scatter.19
  1195.1 176.5 all-reduce.2
where the time goes:
time: 1400 us
  waiting for transfers between devices  1080 us (77%)
  matrix products  157 us (11%)
  blocking collectives  61.4 us (4%)
  other arithmetic  53.9 us (4%)
  local copies, waits for them, and re-layouts  31.1 us (2%)
  between operations  15.1 us (1%)
    reduce_scatter x5, waiting for transfers between devices, body(): lax.psum_scatter(term_fn(jnp.int32(0), lax.axis_size('grp') * shard_len),...  535 us
    psum x1, waiting for transfers between devices, body(): summed = lax.psum(reduced, 'own')  139 us
    reduce_scatter x1, waiting for transfers between devices, body(): lax.psum_scatter(jnp.stack(value_grads, axis=0), 'grp', scatter_dimension...  90 us
    all_gather x1, waiting for transfers between devices, body(): lax.all_gather(w_down, 'grp', axis=0, tiled=True)  76.1 us
    all_gather x1, waiting for transfers between devices, body(): lax.all_gather(key_local, 'grp', axis=1, tiled=True)  60.6 us
    reduce_scatter x1, waiting for transfers between devices, body(): lax.psum_scatter(jnp.stack(key_grads, axis=0), 'grp', scatter_dimension=1...  51.5 us
    all_gather x1, waiting for transfers between devices, body(): lax.all_gather(w_qkv, 'grp', axis=0, tiled=True)  50.5 us
    psum x1, blocking collectives, body(): summed = lax.psum(reduced, 'own')  39.6 us
  transfers between devices with their start and end apart: 14, of which 14 were waited for; matrix products, arithmetic and copies ran while one was open for 14% of the time, Pallas kernels for 0%

commit v1 on v0

v1 whole, which is shorter than its diff:
```python
import math

import jax
import jax.numpy as jnp
from jax import lax
from jax.experimental import pallas as pl
from jax.experimental.pallas import tpu as pltpu
from jax.sharding import PartitionSpec as P

HEADS = 16
HD = 64
ROT = 16
STEP = 5
BLK = 256
QBLK = 512
KBLK = 512

norm_eps = 1e-05
adam_beta = 0.5
adam_eps = 1e-08
weight_decay = 0.01
learn_rates = (0.02, 0.1, 0.02, 0.01, 0.2)
scale = 1.0 / math.sqrt(HD)
log2e = 1.4426950408889634
soft_mul = scale * log2e
f32 = jnp.float32
low = jnp.bfloat16

erfc_terms = (
    0.17087277,
    -0.82215223,
    1.48851587,
    -1.13520398,
    0.27886807,
    -0.18628806,
    0.09678418,
    0.37409196,
    1.00002368,
    -1.26551223,
)


def params(limit=56):
    return pltpu.CompilerParams(
        dimension_semantics=("arbitrary",), vmem_limit_bytes=limit * 1024 * 1024
    )


def cost(micros):
    return pl.CostEstimate(
        flops=int(micros * 1e8), bytes_accessed=int(micros * 3e5), transcendentals=0
    )


def mm(left, right):
    return lax.dot_general(left, right, (((1,), (0,)), ((), ())), preferred_element_type=f32)


def mm_nt(left, right):
    return lax.dot_general(left, right, (((1,), (1,)), ((), ())), preferred_element_type=f32)


def mm_tn(left, right):
    return lax.dot_general(left, right, (((0,), (0,)), ((), ())), preferred_element_type=f32)


def whole(shape):
    return pl.BlockSpec(shape, lambda i, *_: (0,) * len(shape))


unread = pl.BlockSpec(memory_space=pl.ANY)


def normalize(inputs):
    center = inputs - jnp.mean(inputs, axis=-1, keepdims=True)
    inverse = lax.rsqrt(jnp.mean(center * center, axis=-1, keepdims=True) + norm_eps)
    return (center * inverse, inverse)


def norm_back(grad_norm, normed, inverse):
    mean_one = jnp.mean(grad_norm, axis=-1, keepdims=True)
    mean_two = jnp.mean(grad_norm * normed, axis=-1, keepdims=True)
    return inverse * (grad_norm - mean_one - normed * mean_two)


def turn(tensor, cos_full, sin_front, sin_back, direction):
    ahead = pltpu.roll(tensor, 120, 1)
    behind = pltpu.roll(tensor, 8, 1)
    return tensor * cos_full + direction * (ahead * sin_front + behind * sin_back)


def gelu_parts(pre):
    size = jnp.abs(pre) * math.sqrt(0.5)
    inv = 1.0 / (1.0 + 0.5 * size)
    poly = jnp.full_like(pre, erfc_terms[0])
    for term in erfc_terms[1:]:
        poly = poly * inv + term
    square = size * size
    tail = 0.5 * inv * jnp.exp(poly - square)
    cdf = jnp.where(pre >= 0.0, 1.0 - tail, tail)
    bell = jnp.exp(-square) * (1.0 / math.sqrt(2.0 * math.pi))
    return pre * cdf, cdf + pre * bell


def enter_kernel(
    x_ref, w_ref, rows_ref, bq_ref, bu_ref, cos_ref, sf_ref, sb_ref,
    *rest
):
    q_ref, k_ref, v_ref, kt_ref, vt_ref, n1_ref, n2_ref, act_ref, slope_ref, cols_ref = rest[-10:]

    @pl.when(pl.program_id(0) == 0)
    def _():
        for g in range(w_ref.shape[1]):
            for u in range(w_ref.shape[0]):
                top = g * 128 + u * 16
                cols_ref[top : top + 16, :] = w_ref[u, g]

    normed, _ = normalize(x_ref[...].astype(f32))
    n1 = (normed * rows_ref[0:1] + rows_ref[1:2]).astype(low)
    n2 = (normed * rows_ref[2:3] + rows_ref[3:4]).astype(low)
    n1_ref[...] = n1
    n2_ref[...] = n2
    part = q_ref.shape[1]
    ff = act_ref.shape[1]
    proj = mm(n1, cols_ref[:, : 3 * part]) + bq_ref[...]
    tables = (cos_ref[...], sf_ref[...], sb_ref[...])
    q_ref[...] = turn(proj[:, :part], *tables, 1.0).astype(low)
    key = turn(proj[:, part : 2 * part], *tables, 1.0)
    value = proj[:, 2 * part :]
    k_ref[...] = key.astype(low)
    v_ref[...] = value.astype(low)
    kt_ref[0] = key.T.astype(low)
    vt_ref[0] = value.T.astype(low)
    act, slope = gelu_parts(mm(n2, cols_ref[:, 3 * part : 3 * part + ff]) + bu_ref[...])
    act_ref[...] = act.astype(low)
    slope_ref[...] = slope


def enter(x_row, wide, rows, bias_qkv, bias_up, tables, after):
    seq, width = x_row.shape
    part = bias_qkv.shape[1] // 3
    ff = bias_up.shape[1]
    cols = (width, wide.shape[3])
    steps = seq // BLK
    blk = lambda cols: pl.BlockSpec((BLK, cols), lambda i: (i, 0))
    flip = pl.BlockSpec((1, part, BLK), lambda i: (i, 0, 0))
    shape = jax.ShapeDtypeStruct
    return pl.pallas_call(
        enter_kernel,
        grid=(steps,),
        in_specs=[
            blk(width), whole(wide.shape), whole(rows.shape),
            whole(bias_qkv.shape), whole(bias_up.shape), blk(part), blk(part), blk(part),
        ]
        + [unread] * len(after),
        out_specs=[blk(part)] * 3 + [flip] * 2 + [blk(width)] * 2 + [blk(ff)] * 2 + [whole(cols)],
        out_shape=[shape((seq, part), low)] * 3
        + [shape((steps, part, BLK), low)] * 2
        + [shape((seq, width), low)] * 2
        + [shape((seq, ff), low), shape((seq, ff), f32), shape(cols, low)],
        compiler_params=params(),
        cost_estimate=cost(17),
        name="enter",
    )(x_row, wide, rows, bias_qkv, bias_up, *tables, *after)


def split_heads(block):
    lane = lax.broadcasted_iota(jnp.int32, block.shape, 1)
    wide = block.astype(f32)
    return (
        jnp.where(lane < HD, wide, 0.0).astype(low),
        jnp.where(lane >= HD, wide, 0.0).astype(low),
    )


def allowed_keys(kseg_ref, qinfo_ref, j, i):
    key_part = kseg_ref[pl.ds(j * KBLK, KBLK), :]
    key_seg = jnp.concatenate([key_part] * (QBLK // 128), axis=1)
    key_pos = lax.broadcasted_iota(jnp.int32, (KBLK, QBLK), 0) + j * KBLK
    query_pos = lax.broadcasted_iota(jnp.int32, (KBLK, QBLK), 1) + i * QBLK
    same = (key_seg == qinfo_ref[0, 0:1, :]) | (key_seg == qinfo_ref[0, 1:2, :]) | (key_seg == 0)
    return same & (key_pos <= query_pos)


def fold_rows(tile, how):
    return how(tile.reshape(tile.shape[0] // 8, 8, tile.shape[1]), axis=0)


def each_block(i, trunk, count, run):
    def step(j, carry):
        end = (j + 1) * KBLK
        open_block = (end <= i * QBLK) & (end <= trunk)

        @pl.when(open_block)
        def _():
            run(j, False)

        @pl.when(jnp.logical_not(open_block))
        def _():
            run(j, True)

        return carry

    lax.fori_loop(0, count, step, 0)


def forward_kernel(
    trunk_ref, q_ref, k_ref, vt_ref, qinfo_ref, kseg_ref,
    attn_ref, lse_ref, s_scr, m_scr, l_scr, o_scr,
):
    i = pl.program_id(0)
    heads = split_heads(q_ref[...])
    count = i * QBLK // KBLK + 1
    m_scr[...] = jnp.full(m_scr.shape, -3e38, f32)

    def scores(j, masked):
        keys = k_ref[pl.ds(j * KBLK, KBLK), :]
        allowed = allowed_keys(kseg_ref, qinfo_ref, j, i) if masked else None
        for h in range(2):
            tile = mm_nt(keys, heads[h])
            if masked:
                tile = jnp.where(allowed, tile, -1e30)
            s_scr[h, j] = tile
            m_scr[h] = jnp.maximum(m_scr[h], fold_rows(tile, jnp.max))

    each_block(i, trunk_ref[0], count, scores)
    tops = [jnp.max(m_scr[h], axis=0, keepdims=True) * soft_mul for h in range(2)]
    l_scr[...] = jnp.zeros(l_scr.shape, f32)

    def exps(j, carry):
        for h in range(2):
            tile = jnp.exp2(s_scr[h, j] * soft_mul - tops[h])
            s_scr[h, j] = tile
            l_scr[h] += fold_rows(tile, jnp.sum)
        return carry

    lax.fori_loop(0, count, exps, 0)
    sums = [jnp.sum(l_scr[h], axis=0, keepdims=True) for h in range(2)]
    invs = [1.0 / total for total in sums]
    for h in range(2):
        lse_ref[0, h : h + 1, :] = tops[h] + jnp.log(sums[h]) * log2e
    o_scr[...] = jnp.zeros(o_scr.shape, f32)

    def weigh(j, carry):
        for h in range(2):
            probs = (s_scr[h, j] * invs[h]).astype(low)
            rows = slice(h * HD, (h + 1) * HD)
            o_scr[rows, :] += mm(vt_ref[2 * j, rows, :], probs[:BLK]) + mm(
                vt_ref[2 * j + 1, rows, :], probs[BLK:]
            )
        return carry

    lax.fori_loop(0, count, weigh, 0)
    attn_ref[...] = o_scr[...].T.astype(low)


def attend_forward(trunk, q, k, vt, qinfo, kseg):
    seq, part = q.shape
    steps = seq // QBLK
    blk = pl.BlockSpec((QBLK, part), lambda i, t: (i, 0))
    info = pl.BlockSpec((1, 8, QBLK), lambda i, t: (i, 0, 0))
    shape = jax.ShapeDtypeStruct
    return pl.pallas_call(
        forward_kernel,
        grid_spec=pltpu.PrefetchScalarGridSpec(
            num_scalar_prefetch=1,
            grid=(steps,),
            in_specs=[blk, whole(k.shape), whole(vt.shape), info, whole(kseg.shape)],
            out_specs=[blk, info],
            scratch_shapes=[
                pltpu.VMEM((2, seq // KBLK, KBLK, QBLK), f32),
                pltpu.VMEM((2, 8, QBLK), f32),
                pltpu.VMEM((2, 8, QBLK), f32),
                pltpu.VMEM((part, QBLK), f32),
            ],
        ),
        out_shape=[shape((seq, part), low), shape((steps, 8, QBLK), f32)],
        compiler_params=params(),
        cost_estimate=cost(19),
        name="attend_forward",
    )(trunk, q, k, vt, qinfo, kseg)


def merge_kernel(place_ref, attn_ref, act_ref, wo_ref, wd_ref, out_ref):
    out = mm(attn_ref[...], wo_ref[...]) + mm(act_ref[...], wd_ref[...])
    store_pair(out_ref, out.astype(low), place_ref[0])


def store_pair(ref, value, place):
    near = place % 2
    ref[0, near, 0] = value[:BLK]
    ref[0, 1 - near, 0] = value[BLK:]


def by_distance(width):
    def index(i, t):
        apart = jnp.bitwise_xor(i, lax.div(t[0], 2))
        return lax.rem(apart, 2), 0, lax.div(apart, 2), 0, 0

    return pl.BlockSpec((1, 2, 1, BLK, width), index)


def merge_out(place, attn, act, w_out, w_down):
    seq, part = attn.shape
    ff = act.shape[1]
    width = w_out.shape[1]
    blk = lambda cols: pl.BlockSpec((2 * BLK, cols), lambda i, t: (i, 0))
    return pl.pallas_call(
        merge_kernel,
        grid_spec=pltpu.PrefetchScalarGridSpec(
            num_scalar_prefetch=1,
            grid=(seq // (2 * BLK),),
            in_specs=[blk(part), blk(ff), whole(w_out.shape), whole(w_down.shape)],
            out_specs=by_distance(width),
        ),
        out_shape=jax.ShapeDtypeStruct((2, 2, 2, BLK, width), low),
        compiler_params=params(),
        cost_estimate=cost(7),
        name="merge_out",
    )(place, attn, act, w_out, w_down)


def cotangent_kernel(
    c_ref, attn_ref, act_ref, slope_ref, n2_ref, wo_ref, wd_ref, _,
    ga_ref, gp_ref, pieces_ref, csum_ref, psum_ref, _out, up_scr, od_scr,
):
    i = pl.program_id(0)

    @pl.when(i == 0)
    def _():
        up_scr[...] = jnp.zeros(up_scr.shape, f32)
        od_scr[...] = jnp.zeros(od_scr.shape, f32)
        csum_ref[...] = jnp.zeros(csum_ref.shape, f32)
        psum_ref[...] = jnp.zeros(psum_ref.shape, f32)

    c = c_ref[...]
    ga_ref[...] = mm_nt(c, wo_ref[...]).astype(low)
    gp = (mm_nt(c, wd_ref[...]) * slope_ref[...]).astype(low)
    gp_ref[...] = gp
    csum_ref[...] += fold_rows(c.astype(f32), jnp.sum)
    psum_ref[...] += fold_rows(gp.astype(f32), jnp.sum)
    part = attn_ref.shape[1]
    od_scr[:part, :] += mm_tn(attn_ref[...], c)
    od_scr[part:, :] += mm_tn(act_ref[...], c)
    up_scr[...] += mm_tn(n2_ref[...], gp)

    @pl.when(i == pl.num_programs(0) - 1)
    def _():
        for o in range(16):
            rg, ch = divmod(o, 2)
            for g in range(8):
                pieces_ref[o, g * 16 : (g + 1) * 16, :] = up_scr[
                    g * 128 + rg * 16 : g * 128 + (rg + 1) * 16, ch * 256 : (ch + 1) * 256
                ]
            for b in range(4):
                pieces_ref[o, 128 + b * 32 : 160 + b * 32, :] = od_scr[
                    part + o * 32 : part + (o + 1) * 32, b * 256 : (b + 1) * 256
                ]
            for b in range(2):
                lane = ch * 512 + b * 256
                pieces_ref[o, 256 + b * 16 : 272 + b * 16, :] = od_scr[
                    rg * 16 : (rg + 1) * 16, lane : lane + 256
                ]


def cotangent_side(c_row, attn, act, slope, n2, w_out, w_down, late):
    seq, width = c_row.shape
    part = attn.shape[1]
    ff = act.shape[1]
    blk = lambda cols: pl.BlockSpec((2 * BLK, cols), lambda i: (i, 0))
    shape = jax.ShapeDtypeStruct
    return pl.pallas_call(
        cotangent_kernel,
        grid=(seq // (2 * BLK),),
        in_specs=[
            blk(width), blk(part), blk(ff), blk(ff), blk(width), whole(w_out.shape),
            whole(w_down.shape), unread,
        ],
        out_specs=[
            blk(part), blk(ff), whole((16, 288, 256)), whole((8, width)), whole((8, ff)), unread,
        ],
        out_shape=[
            shape((seq, part), low), shape((seq, ff), low), shape((16, 288, 256), f32),
            shape((8, width), f32), shape((8, ff), f32), shape(late.shape, late.dtype),
        ],
        scratch_shapes=[pltpu.VMEM((width, ff), f32), pltpu.VMEM((part + ff, width), f32)],
        input_output_aliases={7: 5},
        compiler_params=params(),
        cost_estimate=cost(14),
        name="cotangent_side",
    )(c_row, attn, act, slope, n2, w_out, w_down, late)


def backward_kernel(
    trunk_ref, q_ref, k_ref, v_ref, kt_ref, ga_ref, lse_ref, qinfo_ref, kseg_ref,
    cos_ref, sf_ref, sb_ref, *rest
):
    gqkv_ref, p_scr, dp_scr, dk_scr, dv_scr, dq_scr, d_scr = rest[-7:]
    i = pl.num_programs(0) - 1 - pl.program_id(0)

    @pl.when(pl.program_id(0) == 0)
    def _():
        dk_scr[...] = jnp.zeros(dk_scr.shape, f32)
        dv_scr[...] = jnp.zeros(dv_scr.shape, f32)

    heads = split_heads(q_ref[...])
    grads = split_heads(ga_ref[...])
    q_pair = jnp.concatenate(heads, axis=0)
    g_pair = jnp.concatenate(grads, axis=0)
    count = i * QBLK // KBLK + 1
    d_scr[...] = jnp.zeros(d_scr.shape, f32)

    def probs_of(j, masked):
        rows = pl.ds(j * KBLK, KBLK)
        keys = k_ref[rows, :]
        values = v_ref[rows, :]
        allowed = allowed_keys(kseg_ref, qinfo_ref, j, i) if masked else None
        for h in range(2):
            tile = jnp.exp2(mm_nt(keys, heads[h]) * soft_mul - lse_ref[0, h : h + 1, :])
            if masked:
                tile = jnp.where(allowed, tile, 0.0)
            back = mm_nt(values, grads[h])
            p_scr[h, j] = tile
            dp_scr[h, j] = back
            d_scr[h] += fold_rows(tile * back, jnp.sum)

    each_block(i, trunk_ref[0], count, probs_of)
    deltas = [jnp.sum(d_scr[h], axis=0, keepdims=True) for h in range(2)]
    dq_scr[...] = jnp.zeros(dq_scr.shape, f32)

    def push(j, carry):
        lows = []
        scores = []
        for h in range(2):
            probs = p_scr[h, j]
            ds = (probs * (dp_scr[h, j] - deltas[h])).astype(low)
            lows.append(probs.astype(low))
            scores.append(ds)
            part = slice(h * HD, (h + 1) * HD)
            dq_scr[part, :] += mm(kt_ref[2 * j, part, :], ds[:BLK]) + mm(
                kt_ref[2 * j + 1, part, :], ds[BLK:]
            )
        rows = pl.ds(j * KBLK, KBLK)
        dk_scr[rows, :] += mm(jnp.concatenate(scores, axis=1), q_pair)
        dv_scr[rows, :] += mm(jnp.concatenate(lows, axis=1), g_pair)
        return carry

    lax.fori_loop(0, count, push, 0)
    tables = (cos_ref[...], sf_ref[...], sb_ref[...])
    rows = pl.ds(i * QBLK, QBLK)
    part = q_ref.shape[1]
    gqkv_ref[:, :part] = turn(dq_scr[...].T * scale, *tables, -1.0).astype(low)
    gqkv_ref[:, part : 2 * part] = turn(dk_scr[rows, :] * scale, *tables, -1.0).astype(low)
    gqkv_ref[:, 2 * part :] = dv_scr[rows, :].astype(low)


def attend_backward(trunk, q, k, v, kt, grad_attn, lse, qinfo, kseg, tables, after):
    seq, part = q.shape
    steps = seq // QBLK
    last = steps - 1
    blk = lambda cols: pl.BlockSpec((QBLK, cols), lambda i, t: (last - i, 0))
    info = pl.BlockSpec((1, 8, QBLK), lambda i, t: (last - i, 0, 0))
    return pl.pallas_call(
        backward_kernel,
        grid_spec=pltpu.PrefetchScalarGridSpec(
            num_scalar_prefetch=1,
            grid=(steps,),
            in_specs=[
                blk(part), whole(k.shape), whole(v.shape), whole(kt.shape), blk(part), info, info,
                whole(kseg.shape), blk(part), blk(part), blk(part),
            ]
            + [unread] * len(after),
            out_specs=blk(3 * part),
            scratch_shapes=[
                pltpu.VMEM((2, seq // KBLK, KBLK, QBLK), f32),
                pltpu.VMEM((2, seq // KBLK, KBLK, QBLK), f32),
                pltpu.VMEM((seq, part), f32),
                pltpu.VMEM((seq, part), f32),
                pltpu.VMEM((part, QBLK), f32),
                pltpu.VMEM((2, 8, QBLK), f32),
            ],
        ),
        out_shape=jax.ShapeDtypeStruct((seq, 3 * part), low),
        compiler_params=params(),
        cost_estimate=cost(26),
        name="attend_backward",
    )(trunk, q, k, v, kt, grad_attn, lse, qinfo, kseg, *tables, *after)


def leave_kernel(
    place_ref, gqkv_ref, gp_ref, x_ref, n1_ref, cols_ref, rows_ref, csum_ref, psum_ref, *rest
):
    h_ref, keep_ref, send_ref, g_scr, v_scr, qsum_scr = rest[-6:]
    i = pl.program_id(0)
    part = gqkv_ref.shape[1]
    ff = gp_ref.shape[1]

    @pl.when(i == 0)
    def _():
        g_scr[...] = jnp.zeros(g_scr.shape, f32)
        v_scr[...] = jnp.zeros(v_scr.shape, f32)
        qsum_scr[...] = jnp.zeros(qsum_scr.shape, f32)

    gqkv = gqkv_ref[...]
    normed, _ = normalize(x_ref[...].astype(f32))
    one = mm_nt(gqkv, cols_ref[:, :part])
    two = mm_nt(gp_ref[...], cols_ref[:, part : part + ff])
    store_pair(h_ref, (one * rows_ref[0:1] + two * rows_ref[2:3]).astype(low), place_ref[0])
    v_scr[0] += fold_rows(one * normed, jnp.sum)
    v_scr[1] += fold_rows(one, jnp.sum)
    v_scr[2] += fold_rows(two * normed, jnp.sum)
    v_scr[3] += fold_rows(two, jnp.sum)
    qsum_scr[...] += fold_rows(gqkv.astype(f32), jnp.sum)
    g_scr[:, :part] += mm_tn(n1_ref[...], gqkv)

    @pl.when(i == pl.num_programs(0) - 1)
    def _():
        place = place_ref[0]
        width = csum_ref.shape[1]
        lane = lax.broadcasted_iota(jnp.int32, (1, width), 1)
        mine = (lane >= place * 128) & (lane < (place + 1) * 128)
        near = (lane >= (place % 2) * 512) & (lane < (place % 2 + 1) * 512)
        qsum = jnp.sum(qsum_scr[...], axis=0, keepdims=True)
        csum = jnp.where(mine, jnp.sum(csum_ref[...], axis=0, keepdims=True), 0.0)
        psum = jnp.sum(psum_ref[...], axis=0, keepdims=True)
        psum = jnp.where(near, jnp.concatenate([psum] * 2, axis=1), 0.0)
        rows = [jnp.sum(v_scr[n], axis=0, keepdims=True) for n in range(4)]
        for n in range(3):
            spread = jnp.concatenate([qsum[:, n * 128 : (n + 1) * 128]] * 8, axis=1)
            rows.append(jnp.where(mine, spread, 0.0))
        rows += [csum, csum]
        for n in range(4):
            rows.append(jnp.where(place // 2 == n, psum, 0.0))
        rows.append(jnp.zeros((128 - len(rows), width), f32))
        g_scr[:, part:] = jnp.concatenate(rows, axis=0).T
        for out_ref, ch in ((keep_ref, place_ref[1]), (send_ref, 1 - place_ref[1])):
            lanes = pl.ds(pl.multiple_of(ch * 256, 256), 256)
            for rg in range(8):
                for g in range(8):
                    top = g * 128 + rg * 16
                    out_ref[rg, g * 16 : (g + 1) * 16, :] = g_scr[top : top + 16, lanes]


def leave(place, gqkv, grad_pre, x_row, n1, cols, rows, csum, psum, after):
    seq, width = x_row.shape
    part3 = gqkv.shape[1]
    ff = grad_pre.shape[1]
    steps = seq // (2 * BLK)
    blk = lambda cols: pl.BlockSpec((2 * BLK, cols), lambda i, t: (i, 0))
    shape = jax.ShapeDtypeStruct
    return pl.pallas_call(
        leave_kernel,
        grid_spec=pltpu.PrefetchScalarGridSpec(
            num_scalar_prefetch=1,
            grid=(steps,),
            in_specs=[
                blk(part3), blk(ff), blk(width), blk(width), whole(cols.shape),
                whole(rows.shape), whole(csum.shape), whole(psum.shape),
            ]
            + [unread] * len(after),
            out_specs=[by_distance(width), whole((8, 128, 256)), whole((8, 128, 256))],
            scratch_shapes=[
                pltpu.VMEM((width, part3 + 128), f32),
                pltpu.VMEM((4, 8, width), f32),
                pltpu.VMEM((8, part3), f32),
            ],
        ),
        out_shape=[
            shape((2, 2, 2, BLK, width), low), shape((8, 128, 256), f32),
            shape((8, 128, 256), f32),
        ],
        compiler_params=params(),
        cost_estimate=cost(300),
        name="leave",
    )(place, gqkv, grad_pre, x_row, n1, cols, rows, csum, psum, *after)


def two_summands(tail):
    lane = lax.broadcasted_iota(jnp.int32, tail.shape, 1)
    head = tail.astype(low).astype(f32)
    rest = pltpu.roll(tail - head, 16, 1)
    return jnp.where(lane < 16, head, jnp.where(lane < 32, rest, 0.0)).astype(low)


def pair_kernel(core_ref, keep_ref, got_ref, *rest):
    out_ref = rest[-1]
    for n in range(keep_ref.shape[0]):
        total = keep_ref[n] + got_ref[n]
        out_ref[n] = total.astype(low)

        if total.shape[0] == 128:

            @pl.when(core_ref[0] == 1)
            def _(n=n, total=total):
                out_ref[n, :, 128:] = two_summands(total[:, 128:])


def sum_kernel(core_ref, got_ref, *rest):
    out_ref = rest[-1]
    total = jnp.sum(got_ref[...].astype(f32), axis=0)
    out_ref[...] = total.astype(low)

    if total.shape[0] == 128:

        @pl.when(core_ref[0] == 1)
        def _():
            tail = total[:, 128:]
            out_ref[:, 128:] = two_summands(tail + pltpu.roll(tail, 112, 1))


def pack_kernel(block_ref, *rest):
    for n in range(rest[-1].shape[0]):
        rest[-1][n] = block_ref[...]


def copies_of(block, count, after):
    return pl.pallas_call(
        pack_kernel,
        grid=(2,),
        in_specs=[whole(block.shape)] + [unread] * len(after),
        out_specs=pl.BlockSpec((count // 2,) + block.shape, lambda i: (i, 0, 0)),
        out_shape=jax.ShapeDtypeStruct((count,) + block.shape, block.dtype),
        compiler_params=params(),
        cost_estimate=cost(2),
        name="copies_of",
    )(block, *after)


def far_kernel(parts_ref, _, out_ref):
    out_ref[...] = parts_ref[0]


def far_blocks(parts, before):
    _, _, depth, local_len, width = parts.shape
    rows = local_len // 2
    return pl.pallas_call(
        far_kernel,
        grid=(2,),
        in_specs=[
            pl.BlockSpec((1, 1, depth, rows, width), lambda i: (1, 0, 0, i, 0)), unread,
        ],
        out_specs=pl.BlockSpec((1, depth, rows, width), lambda i: (0, 0, i, 0)),
        out_shape=jax.ShapeDtypeStruct((1,) + parts.shape[2:], parts.dtype),
        compiler_params=params(),
        cost_estimate=cost(2),
        name="far_blocks",
    )(parts, before)


def pair_sum(core, keep, got, after):
    count, rows, lanes = keep.shape
    block = pl.BlockSpec((count // 4, rows, lanes), lambda i, t: (i, 0, 0))
    return pl.pallas_call(
        pair_kernel,
        grid_spec=pltpu.PrefetchScalarGridSpec(
            num_scalar_prefetch=1,
            grid=(4,),
            in_specs=[block, block] + [unread] * len(after),
            out_specs=block,
        ),
        out_shape=jax.ShapeDtypeStruct(keep.shape, low),
        compiler_params=params(),
        cost_estimate=cost(4),
        name="pair_sum",
    )(core, keep, got, *after)


def sum_pieces(core, got, after):
    owners, rows, lanes = got.shape
    return pl.pallas_call(
        sum_kernel,
        grid_spec=pltpu.PrefetchScalarGridSpec(
            num_scalar_prefetch=1,
            grid=(1,),
            in_specs=[whole(got.shape)] + [unread] * len(after),
            out_specs=whole((rows, lanes)),
        ),
        out_shape=jax.ShapeDtypeStruct((rows, lanes), low),
        compiler_params=params(),
        cost_estimate=cost(2),
        name="sum_pieces",
    )(core, got, *after)


def branch_of(segment):
    return jnp.where(segment >= 5, 1 + (segment - 5) // 2, segment)


def rotary_tables(seq):
    lane = jnp.arange(128) % HD
    front = lane < ROT // 2
    back = (lane >= ROT // 2) & (lane < ROT)
    inv_freq = 10000.0 ** (-(2 * (lane % (ROT // 2))).astype(f32) / ROT)
    inv_freq = jnp.where(front | back, inv_freq, 0.0)
    angles = jnp.arange(seq).astype(f32)[:, None] * inv_freq[None, :]
    sines = jnp.sin(angles)
    return jnp.cos(angles), jnp.where(front, -sines, 0.0), jnp.where(back, sines, 0.0)


def tree_info(segment, live):
    seq = segment.shape[0]
    steps = seq // QBLK
    trunk = jnp.sum((segment == 0).astype(jnp.int32)).reshape(1)
    key_seg = jnp.broadcast_to(jnp.where(live == 1, segment, -1)[:, None], (seq, 128))
    pair = jnp.stack([segment, branch_of(segment)]).reshape(2, steps, QBLK).transpose(1, 0, 2)
    return trunk, jnp.pad(pair, ((0, 0), (0, 6), (0, 0))), key_seg


def adam_store(grad, master, first, second, rate, outs, where):
    new_master, new_first, new_second = adamw_apply(master, first, second, grad, rate)
    for ref, value in zip(outs, (new_master, new_first, new_second, new_master.astype(low))):
        ref[where] = value


def adamw_apply(master, first_mom, second_mom, gradient, learn_rate):
    first_new = adam_beta * first_mom + (1.0 - adam_beta) * gradient
    second_new = adam_beta * second_mom + (1.0 - adam_beta) * gradient * gradient
    correction = 1.0 - adam_beta**STEP
    adam_step = first_new / correction / (jnp.sqrt(second_new / correction) + adam_eps)
    master_new = master - learn_rate * (adam_step + weight_decay * master)
    return (master_new, first_new, second_new)


def adam_call(name, core, pieces, g_spec, states, block, steps, cut, rate):
    def kernel(core_ref, mine_ref, theirs_ref, m_ref, f_ref, s_ref, *outs):
        for half in range(2):
            for cols, pick in cut(pl.program_id(0), half):
                grad = jnp.where(
                    core_ref[0] == half, pick(mine_ref).astype(f32), pick(theirs_ref).astype(f32)
                )
                where = (slice(None), cols)
                adam_store(grad, m_ref[where], f_ref[where], s_ref[where], rate, outs, where)

    tab = pl.BlockSpec(block, lambda i, t: (0, i))
    shape = states[0].shape
    size = shape[0] * shape[1]
    return pl.pallas_call(
        kernel,
        grid_spec=pltpu.PrefetchScalarGridSpec(
            num_scalar_prefetch=1,
            grid=(steps,),
            in_specs=[g_spec] * 2 + [tab] * 3,
            out_specs=[tab] * 4,
        ),
        out_shape=[jax.ShapeDtypeStruct(shape, f32)] * 3 + [jax.ShapeDtypeStruct(shape, low)],
        compiler_params=params(),
        cost_estimate=cost(7),
        name=name,
    )(core, *pieces, *states)


def take(rows):
    return lambda ref: ref[:, rows, :].reshape(-1, ref.shape[2])


def update_up(core, pieces, states, rate):
    def cut(step, half):
        for s in range(2):
            lane = s * 512 + half * 256
            yield slice(lane, lane + 256), take(slice(s * 16, (s + 1) * 16))

    spec = pl.BlockSpec((8, 32, 256), lambda i, t: (0, i, 0))
    return adam_call("update_up", core, pieces, spec, states, (128, 1024), 4, cut, rate)


def update_out(core, pieces, states, rate):
    def cut(step, half):
        for b in range(2):
            lane = half * 512 + b * 256
            yield slice(lane, lane + 256), take(slice(b * 16, (b + 1) * 16))

    spec = pl.BlockSpec((8, 32, 256), lambda i, t: (0, 8, 0))
    return adam_call("update_out", core, pieces, spec, states, (128, 1024), 1, cut, rate)


def update_down(core, pieces, states, rate):
    def kernel(core_ref, mine_ref, theirs_ref, m_ref, f_ref, s_ref, *outs):
        for rg in range(8):
            for half in range(2):
                where = (slice(rg * 64 + half * 32, rg * 64 + half * 32 + 32), slice(None))
                grad = jnp.where(
                    core_ref[0] == half, mine_ref[rg].astype(f32), theirs_ref[rg].astype(f32)
                )
                adam_store(grad, m_ref[where], f_ref[where], s_ref[where], rate, outs, where)

    g_spec = pl.BlockSpec((8, 32, 256), lambda i, t: (0, 4 + i, 0))
    tab = pl.BlockSpec((512, 256), lambda i, t: (0, i))
    shape = states[0].shape
    size = shape[0] * shape[1]
    return pl.pallas_call(
        kernel,
        grid_spec=pltpu.PrefetchScalarGridSpec(
            num_scalar_prefetch=1,
            grid=(4,),
            in_specs=[g_spec] * 2 + [tab] * 3,
            out_specs=[tab] * 4,
        ),
        out_shape=[jax.ShapeDtypeStruct(shape, f32)] * 3 + [jax.ShapeDtypeStruct(shape, low)],
        compiler_params=params(),
        cost_estimate=cost(7),
        name="update_down",
    )(core, *pieces, *states)


def update_qkv(core, pieces, states, rate):
    def kernel(core_ref, mine_ref, theirs_ref, m_ref, f_ref, s_ref, *outs):
        is_mine = core_ref[0] == pl.program_id(0) // 2
        for src in range(8):
            where = (slice(None), slice(src * 128, (src + 1) * 128))
            pick = take(slice(src * 16, (src + 1) * 16))
            grad = jnp.where(is_mine, pick(mine_ref).astype(f32), pick(theirs_ref).astype(f32))
            adam_store(grad, m_ref[where], f_ref[where], s_ref[where], rate, outs, where)

    g_spec = pl.BlockSpec((8, 128, 128), lambda i, t: (0, 0, i % 2))
    tab = pl.BlockSpec((128, 1024), lambda i, t: (0, i))
    shape = states[0].shape
    size = shape[0] * shape[1]
    return pl.pallas_call(
        kernel,
        grid_spec=pltpu.PrefetchScalarGridSpec(
            num_scalar_prefetch=1,
            grid=(3,),
            in_specs=[g_spec] * 2 + [tab] * 3,
            out_specs=[tab] * 4,
        ),
        out_shape=[jax.ShapeDtypeStruct(shape, f32)] * 3 + [jax.ShapeDtypeStruct(shape, low)],
        compiler_params=params(),
        cost_estimate=cost(7),
        name="update_qkv",
    )(core, *pieces, *states)


def fold_kernel(mine_ref, one_ref, two_ref, three_ref, _, keep_ref, send_ref):
    sums = []
    for z in range(2):
        total = mine_ref[0, 0, z].astype(f32)
        for ref in (one_ref, two_ref, three_ref):
            total += ref[0, z].astype(f32)
        sums.append(total)
    keep_ref[...] = sums[0]
    send_ref[...] = sums[1].astype(low)


def fold(parts, got, before):
    _, _, _, local_len, width = parts.shape
    rows = 128
    mine = pl.BlockSpec((1, 1, 2, rows, width), lambda i: (0, 0, 0, i, 0))
    other = pl.BlockSpec((1, 2, rows, width), lambda i: (0, 0, i, 0))
    block = pl.BlockSpec((rows, width), lambda i: (i, 0))
    shape = jax.ShapeDtypeStruct((local_len, width), f32)
    return pl.pallas_call(
        fold_kernel,
        grid=(local_len // rows,),
        in_specs=[mine, other, other, other, unread],
        out_specs=[block, block],
        out_shape=[shape, jax.ShapeDtypeStruct((local_len, width), low)],
        compiler_params=params(),
        cost_estimate=cost(4),
        name="fold",
    )(parts, *got, before)


def finish_out_kernel(keep_ref, got_ref, x_ref, bias_ref, _, out_ref):
    total = keep_ref[...] + got_ref[...].astype(f32)
    out_ref[...] = (x_ref[...].astype(f32) + total + bias_ref[0:1]).astype(low)


def finish_grad_kernel(keep_ref, got_ref, x_ref, c_ref, _, out_ref):
    normed, inverse = normalize(x_ref[...].astype(f32))
    total = keep_ref[...] + got_ref[...].astype(f32)
    out_ref[...] = c_ref[...].astype(f32) + norm_back(total, normed, inverse)


def finish(kernel, name, operands, before, dtype):
    local_len, width = operands[0].shape
    rows = 128
    block = pl.BlockSpec((rows, width), lambda i: (i, 0))
    return pl.pallas_call(
        kernel,
        grid=(local_len // rows,),
        in_specs=[block if o.shape[0] == local_len else whole(o.shape) for o in operands]
        + [unread],
        out_specs=block,
        out_shape=jax.ShapeDtypeStruct((local_len, width), dtype),
        compiler_params=params(),
        cost_estimate=cost(3),
        name=name,
    )(*operands, before)


def body(
    hidden_in,
    cotangent,
    segment_ids,
    live_slots,
    w_qkv,
    w_out,
    w_up,
    w_down,
    w_vec,
    master_qkv,
    master_out,
    master_up,
    master_down,
    master_vec,
    first_qkv,
    first_out,
    first_up,
    first_down,
    first_vec,
    second_qkv,
    second_out,
    second_up,
    second_down,
    second_vec,
):
    grp = ("zl", "x")
    own = ("y", "zh", "core")
    groups = lax.axis_size(grp)
    owners = lax.axis_size(own)
    pos = lax.axis_index(grp)
    _, local_len, width = hidden_in.shape
    seq_len = local_len * groups
    rows = w_qkv.shape[0]
    ff_part = w_up.shape[1] // groups
    qkv_part = 3 * rows
    n_vec = w_vec.shape[1]
    x_local = hidden_in[0]
    c_local = cotangent[0]

    sub = rows // 8
    first = (lax.axis_index("y") * 2 + lax.axis_index("core")) * sub

    def cut(table):
        return lax.dynamic_slice_in_dim(table, first, sub, 0)

    send_w = jnp.concatenate(
        [
            cut(w_qkv).reshape(sub, 3, groups, rows).transpose(2, 0, 1, 3).reshape(groups, sub, qkv_part),
            cut(w_up).reshape(sub, groups, ff_part).transpose(1, 0, 2),
            jnp.broadcast_to(jnp.pad(cut(w_vec), ((0, 0), (0, 128 - n_vec)))[None], (groups, sub, 128)),
        ],
        axis=2,
    )
    part_w = lax.all_to_all(send_w, grp, 0, 0)
    wide = lax.all_to_all(jnp.broadcast_to(part_w[None], (8,) + part_w.shape), ("y", "core"), 0, 0)
    vec_cols = wide[:, :, :, qkv_part + ff_part : qkv_part + ff_part + n_vec]
    vectors = vec_cols.astype(f32).transpose(3, 1, 0, 2).reshape(n_vec, width)
    x_row = lax.all_gather(x_local, grp, axis=0, tiled=True)
    c_row = lax.all_gather(c_local, grp, axis=0, tiled=True)

    gain_rows = jnp.pad(vectors[:4], ((0, 4), (0, 0)))
    bias_qkv = w_vec[:, 4:7].astype(f32).T.reshape(1, qkv_part)
    bias_up = lax.dynamic_slice_in_dim(vectors[9:].reshape(-1), pos * ff_part, ff_part)[None]
    core = lax.axis_index("core").astype(jnp.int32).reshape(1)
    place = jnp.concatenate([pos.astype(jnp.int32).reshape(1), core])
    tables = rotary_tables(seq_len)
    trunk, qinfo, kseg = tree_info(segment_ids[0], live_slots[0])

    q, k, v, kt, vt, n1, n2, act, slope, cols = enter(
        x_row, wide, gain_rows, bias_qkv, bias_up, tables, (kseg, qinfo)
    )
    attn, lse = attend_forward(trunk, q, k, vt, qinfo, kseg)
    out_part = merge_out(place, attn, act, w_out, w_down)
    grad_attn, grad_pre, pieces_a, csum, psum, out_late = cotangent_side(
        c_row, attn, act, slope, n2, w_out, w_down, out_part
    )

    def along_x(block, d):
        return lax.ppermute(block, "x", [(g, g ^ d) for g in range(4)])

    def hand_out(parts, before):
        return [
            along_x(parts[0, 1:2], 1),
            along_x(parts[1, 0:1] if before is None else far_blocks(parts, before), 2),
            along_x(parts[1, 1:2], 3),
        ]

    def add_up(parts, got, before):
        keep, send = fold(parts, got, before)
        return keep, lax.ppermute(send, "zl", [(0, 1), (1, 0)])

    def across(block):
        return lax.ppermute(block, "core", [(0, 1), (1, 0)])

    def turn_over(pieces):
        return lax.all_to_all(pieces, ("y", "zh"), 0, 0)

    def spread(block, after):
        mine = turn_over(copies_of(block, owners // 2, after))
        return mine, across(mine)

    gqkv = attend_backward(trunk, q, k, v, kt, grad_attn, lse, qinfo, kseg, tables, ())
    sum_a = lax.psum_scatter(
        pieces_a.reshape(owners * 288, 256), own, scatter_dimension=0, tiled=True
    ).astype(low)
    got_out = hand_out(out_late, gqkv)
    h_part, keep_b, send_b = leave(
        place, gqkv, grad_pre, x_row, n1, cols, gain_rows, csum, psum, (got_out[0], got_out[2])
    )
    got_h = hand_out(h_part, None)
    got_b = turn_over(pair_sum(core, keep_b, across(send_b), (got_out[1],)))
    sum_b = sum_pieces(core, got_b, ())
    both = jnp.stack([sum_a[:128].reshape(groups, 16, 256), sum_b.reshape(groups, 16, 256)], axis=1)
    turned = lax.all_to_all(both, grp, 0, 0)
    all_a = spread(jnp.concatenate([turned[:, 0].reshape(128, 256), sum_a[128:]], axis=0), got_h[::2])
    all_b = spread(turned[:, 1].reshape(128, 256), (all_a[0], got_h[1]))
    halves = [part[:, :, 128:160].astype(f32) for part in all_b]
    vec_sums = jnp.where(core[0] == 1, halves[0], halves[1]).reshape(8, groups, 16, 32)
    vec_grad = jnp.sum(vec_sums[..., :16] + vec_sums[..., 16:], axis=1).reshape(rows, 16)[:, :n_vec]

    bias_rows = jnp.broadcast_to((vectors[7] + vectors[8])[None], (8, width))
    results = [
        update_qkv(core, all_b, (master_qkv, first_qkv, second_qkv), learn_rates[0]),
        update_out(core, all_a, (master_out, first_out, second_out), learn_rates[1]),
        update_up(core, all_a, (master_up, first_up, second_up), learn_rates[2]),
        update_down(core, all_a, (master_down, first_down, second_down), learn_rates[3]),
    ]
    layer_out = finish(
        finish_out_kernel,
        "finish_out",
        (*add_up(out_late, got_out, all_a[0]), x_local, bias_rows),
        results[1][3],
        low,
    )
    input_grad = finish(
        finish_grad_kernel,
        "finish_grad",
        (*add_up(h_part, got_h, all_b[0]), x_local, c_local),
        results[2][3],
        f32,
    )
    vec_new = adamw_apply(master_vec, first_vec, second_vec, vec_grad, learn_rates[4])
    results.append(vec_new + (vec_new[0].astype(low),))
    return (
        (layer_out[None], input_grad[None])
        + tuple(r[0] for r in results)
        + tuple(r[1] for r in results)
        + tuple(r[2] for r in results)
        + tuple(r[3] for r in results)
    )


def solution(mesh):
    fine = jax.sharding.Mesh(
        mesh.devices.reshape(2, 4, 4, 2, 2), ("zl", "x", "y", "zh", "core")
    )
    grp = ("zl", "x")
    own = ("y", "zh", "core")
    act_spec = P(own, grp, None)
    id_spec = P(own, None)
    tab_spec = P(grp, None)
    return jax.shard_map(
        body,
        mesh=fine,
        in_specs=(act_spec,) * 2 + (id_spec,) * 2 + (tab_spec,) * 20,
        out_specs=(act_spec,) * 2 + (tab_spec,) * 20,
        check_vma=False,
    )
```

time: 1400 us -> 326 us (0.23)
  waiting for transfers between devices: 1080 us -> 64 us
  matrix products: 157 us -> 0 us
  Pallas kernels: 0 us -> 142 us
  other arithmetic: 53.9 us -> 12.2 us
  starting transfers between devices: 1.86 us -> 38.6 us
  blocking collectives: 61.4 us -> 27.3 us
    reduce_scatter x7 -> x1, waiting for transfers between devices: 676 us -> 6.09 us  [body(): lax.psum_scatter(pieces_a.reshape(owners * 288, 256), own, scatter_dimens...]
    all_gather x6 -> x2, waiting for transfers between devices: 260 us -> 14.6 us  [the longest x1 11.6 us: body(): c_row = lax.all_gather(c_local, grp, axis=0, tiled=True)]
    dot_general x36 -> x0, matrix products: 157 us -> none  [the longest x4 27.3 us: product_term(): jnp.einsum('tr,tc->rc', sliced, right_side, preferred_element_type=jnp.fl...]
    pallas_call x0 -> x19, Pallas kernels: none -> 142 us  [the longest x1 24.1 us: attend_backward(): pl.pallas_call(backward_kernel, grid_spec=pltpu.PrefetchScalarGridSpec(nu...]
    psum x1 -> x0, waiting for transfers between devices: 139 us -> none  [body(): summed = lax.psum(reduced, 'own')]
    psum x1 -> x0, blocking collectives: 39.6 us -> none  [body(): summed = lax.psum(reduced, 'own')]
    convert_element_type x12 -> x3, other arithmetic: 29.5 us -> 1.61 us  [the longest x1 0.98 us: body(): sum_a = lax.psum_scatter(pieces_a.reshape(owners * 288, 256), own, scatte...]
    all_to_all x0 -> x2, blocking collectives: none -> 27.3 us  [the longest x1 15 us: turn_over(): return lax.all_to_all(pieces, ('y', 'zh'), 0, 0)]
  transfers between devices with their start and end apart: 14 -> 18, of which waited for: 14 -> 8; matrix products, arithmetic and copies ran while one was open for 14% -> 9% of each run, Pallas kernels for 0% -> 38%
where the time goes in v1:
time: 326 us; the launch traced here: 325 us
  Pallas kernels  142 us (44%)
  waiting for transfers between devices  64 us (20%)
  starting transfers between devices  38.6 us (12%)
  blocking collectives  27.3 us (8%)
  local copies, waits for them, and re-layouts  27 us (8%)
  between operations  14 us (4%)
  other arithmetic  12.2 us (4%)
    pallas_call x1, Pallas kernels, attend_backward(): pl.pallas_call(backward_kernel, grid_spec=pltpu.PrefetchScalarGridSpec(nu...  24.1 us
    all_to_all x1, waiting for transfers between devices, body(): lax.all_to_all(jnp.broadcast_to(part_w[None], (8,) + part_w.shape), ('y',...  17.5 us
    pallas_call x1, Pallas kernels, enter(): pl.pallas_call(enter_kernel, grid=(steps,), in_specs=[blk(width), whole(w...  17.1 us
    ppermute x6, waiting for transfers between devices, along_x(): return lax.ppermute(block, 'x', [(g, g ^ d) for g in range(4)])  16.3 us
    pallas_call x1, Pallas kernels, attend_forward(): pl.pallas_call(forward_kernel, grid_spec=pltpu.PrefetchScalarGridSpec(num...  15.6 us
    pallas_call x1, Pallas kernels, cotangent_side(): pl.pallas_call(cotangent_kernel, grid=(seq // (2 * BLK),), in_specs=[blk(...  15.2 us
    pallas_call x1, Pallas kernels, leave(): pl.pallas_call(leave_kernel, grid_spec=pltpu.PrefetchScalarGridSpec(num_s...  15.2 us
    all_to_all x1, blocking collectives, turn_over(): return lax.all_to_all(pieces, ('y', 'zh'), 0, 0)  15 us
  transfers between devices with their start and end apart: 18, of which 8 were waited for; matrix products, arithmetic and copies ran while one was open for 9% of the time, Pallas kernels for 38%

profile of v1, /device:TPU:1, one launch (start us, length us, event | category | flops | bytes accessed | tf_op | source)
XLA Modules:
  0.0 324.9 jit_solution(6429638835854894436)
XLA Ops:
  10.8 12.3 %all_to_all.30 = bf16[8,16,1024]{2,1,0:T(8,128)(2,1)S(1)} all-to-all(bf16[8,16,1024]{2,1,0:T(8,128)(2,1)S(1)} %copy.59), channel_id=1, replica_groups=mesh['zl'=2,'x'=4,'y'=4,'zh'=2,'core'=2] {'zl','x'}, dimensions={0} | all-to-all | bytes 524288 | tf_op jit(solution)/shard_map/all_to_all | solution.py:945
  23.1 1.6 broadcast_in_dim.60
  24.7 6.5 %all-to-all-start.1 = ((bf16[8,8,16,1024]{3,2,1,0:T(8,128)(2,1)}), bf16[8,8,16,1024]{3,2,1,0:T(8,128)(2,1)S(1)}, u32[]{:S(2)}, u32[]{:S(2)}) async-start(bf16[8,8,16,1024]{3,2,1,0:T(8,128)(2,1)} %broadcast_in_dim.60), calls=%async_computation.1 | async-start | bytes 4194304 | tf_op jit(solution)/shard_map/all_to_all | solution.py:946
  34.4 5.8 %fusion = (f32[2048,128]{1,0:T(8,128)}, f32[2048,128]{1,0:T(8,128)}, f32[2048,128]{1,0:T(8,128)}) fusion(f32[128]{0:T(128)S(1)} %or_select_fusion, f32[2048]{0:T(1024)S(1)} %iota_convert_fusion, pred[128]{0:T(512)(128)(4,1)S(1)} %get-tuple-element.123, pred[128]{0:T(512)(128)(4,1)S(1)} %get-tuple-element.124), kind=kLoop, calls=%fused_computation.2 | loop fusion | flops 1048576 | bytes 3154688 | tf_op jit(solution)/shard_map/jit(_where)/select_n | solution.py:697
  40.2 17.5 %all-to-all-done.1.w_ref = bf16[8,8,16,1024]{3,2,1,0:T(8,128)(2,1)S(1)} async-done(((bf16[8,8,16,1024]{3,2,1,0:T(8,128)(2,1)}), bf16[8,8,16,1024]{3,2,1,0:T(8,128)(2,1)S(1)}, u32[]{:S(2)}, u32[]{:S(2)}) %all-to-all-start.1) | async-done | bytes 2097184 | tf_op jit(solution)/shard_map/all_to_all | solution.py:946
  57.7 1.2 fusion.14
  58.9 1.6 copy.61
  62.6 3.0 all-gather.7.cloned.1.call-done
  65.6 1.3 broadcast_in_dim.67.rest_0_.kseg_ref
  66.9 17.1 %enter.1 = (bf16[2048,128]{1,0:T(8,128)(2,1)}, bf16[2048,128]{1,0:T(8,128)(2,1)}, bf16[2048,128]{1,0:T(8,128)(2,1)}, bf16[8,128,256]{2,1,0:T(8,128)(2,1)}, bf16[...) custom-call(bf16[2048,1024]{1,0:T(8,128)(2,1)} %bitcast.69, ...), custom_call_target="tpu_custom_call" | custom-call | flops 1700000000 | bytes 5100000 | tf_op jit(solution)/shard_map/enter/pallas_call | solution.py:148
  84.0 15.6 %attend_forward.1 = (bf16[2048,128]{1,0:T(8,128)(2,1)}, f32[4,8,512]{2,1,0:T(8,128)}) custom-call(s32[1]{0:T(128)} %bitcast.1.trunk_ref, bf16[2048,128]{1,0:T(8,128)(2,1)} %get-tuple-element.63.q_ref, bf16[2048,128]{1,0:T(8,128)(2,1)} %get-tuple-element.64.k_ref, bf16[8,128,256]{2,1,0:T(8,128)(2,1)} %get-tuple-element.65.vt_ref, ...), custom_call_target="tpu_custom_call" | custom-call | flops 1900000000 | bytes 5700000 | tf_op jit(solution)/shard_map/attend_forward/pallas_call | solution.py:263
  99.6 7.8 %merge_out.1._ = bf16[2,2,2,256,1024]{4,3,2,1,0:T(8,128)(2,1)} custom-call(s32[2]{0:T(128)} %pad_add_fusion.place_ref, bf16[2048,128]{1,0:T(8,128)(2,1)} %get-tuple-element.66.attn_ref, bf16[2048,512]{1,0:T(8,128)(2,1)} %get-tuple-element.67.act_ref, bf16[128,1024]{1,0:T(8,128)(2,1)} %wo_ref.3, bf16[512,1024]{1,0:T(8,128)(2,1)} %wd_ref.3), custom_call_target="tpu_custom_call" | custom-call | flops 700000000 | bytes 2100000 | tf_op jit(solution)/shard_map/merge_out/pallas_call | solution.py:308
  107.3 11.6 %all-gather.5.cloned.1.call-done = bf16[1,2048,1024]{2,1,0:T(8,128)(2,1)} async-done(((bf16[1,256,1024]{2,1,0:T(8,128)(2,1)}), bf16[1,2048,1024]{2,1,0:T(8,128)(2,1)}) %all-gather.5.cloned.1.call-update) | async-done | bytes 4194320 | tf_op jit(solution)/shard_map/all_gather | solution.py:950
  118.9 15.2 %cotangent_side.1 = (bf16[2048,128]{1,0:T(8,128)(2,1)}, bf16[2048,512]{1,0:T(8,128)(2,1)}, f32[16,288,256]{2,1,0:T(8,128)}, f32[8,1024]{1,0:T(8,128)}, f32[8,512...) custom-call(bf16[2048,1024]{1,0:T(8,128)(2,1)} %bitcast.68, ...), custom_call_target="tpu_custom_call", output_to_operand_aliasing={{5}: (7, {})} | custom-call | flops 1400000000 | bytes 4200000 | tf_op jit(solution)/shard_map/cotangent_side/pallas_call | solution.py:372
  134.2 1.7 slice_bitcast_fusion.3
  136.3 24.1 %attend_backward.1._.gqkv_ref = bf16[2048,384]{1,0:T(8,128)(2,1)} custom-call(s32[1]{0:T(128)} %bitcast.1.trunk_ref, bf16[2048,128]{1,0:T(8,128)(2,1)} %get-tuple-element.63.q_ref, bf16[2048,128]{1,0:T(8,128)(2,1)} %get-tuple-element.64.k_ref, bf16[2048,128]{1,0:T(8,128)(2,1)} %get-tuple-element.71.v_ref, bf16[8,128,256]{2,1,0:T(8,128)(2,1)} %get-tuple-element.72.kt_ref, ...), custom_call_target="tpu_custom_call" | custom-call | flops 2600000000 | bytes 7800000 | tf_op jit(solution)/shard_map/attend_backward/pallas_call | solution.py:463
  160.3 2.1 far_blocks.1
  162.4 3.6 %collective-permute-start.1 = (bf16[1,2,256,1024]{3,2,1,0:T(8,128)(2,1)}, bf16[1,2,256,1024]{3,2,1,0:T(8,128)(2,1)S(1)}, u32[]{:S(2)}, u32[]{:S(2)}) collective-permute-start(bf16[1,2,256,1024]{3,2,1,0:T(8,128)(2,1)} %far_blocks.1), channel_id=1, source_target_pairs={{0,32},{16,48},{32,0},{48,16},{1,33},{17,49},{33,1},{49,17},{2,34}... | collective-permute-start | bytes 3145736 | tf_op jit(solution)/shard_map/ppermute | solution.py:970
  167.3 15.2 %leave.1 = (bf16[2,2,2,256,1024]{4,3,2,1,0:T(8,128)(2,1)}, f32[8,128,256]{2,1,0:T(8,128)}, f32[8,128,256]{2,1,0:T(8,128)}) custom-call(s32[2]{0:T(128)} %pad_add_fusion.place_ref, bf16[2048,384]{1,0:T(8,128)(2,1)} %attend_backward.1._.gqkv_ref, bf16[2048,512]{1,0:T(8,128)(2,1)} %get-tuple-element.76.gp_ref, bf16[2048,1024]{1,0:T(8,128)(2,1)} %bitcast.70, ...), custom_call_target="tpu_custom_call" | custom-call | flops 30000001024 | bytes 90000000 | tf_op jit(solution)/shard_map/leave/pallas_call | solution.py:551
  182.5 1.5 collective-permute-start.3
  184.0 4.4 %collective-permute-done.1.rest_0_.two_ref = bf16[1,2,256,1024]{3,2,1,0:T(8,128)(2,1)S(1)} collective-permute-done((bf16[1,2,256,1024]{3,2,1,0:T(8,128)(2,1)}, bf16[1,2,256,1024]{3,2,1,0:T(8,128)(2,1)S(1)}, u32[]{:S(2)}, u32[]{:S(2)}) %collective-permute-start.1) | collective-permute-done | bytes 1048608 | tf_op jit(solution)/shard_map/ppermute | solution.py:970
  189.8 3.8 %pair_sum.1 = bf16[8,128,256]{2,1,0:T(8,128)(2,1)} custom-call(s32[1]{0:T(128)} %bitcast.14.core_ref, f32[8,128,256]{2,1,0:T(8,128)} %get-tuple-element.81.keep_ref, f32[8,128,256]{2,1,0:T(8,128)} %copy-done.11, bf16[1,2,256,1024]{3,2,1,0:T(8,128)(2,1)} %copy-done.9), custom_call_target="tpu_custom_call" | custom-call | flops 400000000 | bytes 1200000 | tf_op jit(solution)/shard_map/pair_sum/pallas_call | solution.py:653
  193.5 6.3 %all-to-all-start.2 = ((bf16[8,128,256]{2,1,0:T(8,128)(2,1)}), bf16[8,128,256]{2,1,0:T(8,128)(2,1)S(1)}, u32[]{:S(2)}, u32[]{:S(2)}) async-start(bf16[8,128,256]{2,1,0:T(8,128)(2,1)} %pair_sum.1), calls=%async_computation.3 | async-start | bytes 1048576 | tf_op jit(solution)/shard_map/all_to_all | solution.py:987
  199.8 3.8 %slice_bitcast_fusion = (bf16[1,2,256,1024]{3,2,1,0:T(8,128)(2,1)}, bf16[1,2,256,1024]{3,2,1,0:T(8,128)(2,1)}, bf16[1,2,256,1024]{3,2,1,0:T(8,128)(2,1)}) fusion(bf16[2,2,2,256,1024]{4,3,2,1,0:T(8,128)(2,1)} %get-tuple-element.83.mine_ref), kind=kLoop, calls=%fused_computation.5 | loop fusion | bytes 6291456 | tf_op jit(solution)/shard_map/squeeze | solution.py:975
  203.6 1.6 collective-permute-start.5
  206.0 5.6 %all-to-all-done.2.got_ref = bf16[8,128,256]{2,1,0:T(8,128)(2,1)S(1)} async-done(((bf16[8,128,256]{2,1,0:T(8,128)(2,1)}), bf16[8,128,256]{2,1,0:T(8,128)(2,1)S(1)}, u32[]{:S(2)}, u32[]{:S(2)}) %all-to-all-start.2) | async-done | bytes 524320 | tf_op jit(solution)/shard_map/all_to_all | solution.py:987
  212.4 1.9 sum_pieces.1
  214.3 6.1 %reduce-scatter.2.cloned.1.call-done = f32[288,256]{1,0:T(8,128)} async-done(((f32[4608,256]{1,0:T(8,128)}), f32[288,256]{1,0:T(8,128)}) %reduce-scatter.2.cloned.1.call-update) | async-done | bytes 294928 | tf_op jit(solution)/shard_map/reduce_scatter | solution.py:994
  221.4 1.5 pad_maximum_fusion.2
  222.9 4.0 %all-to-all-start.3 = ((bf16[8,2,16,256]{3,2,1,0:T(8,128)(2,1)}), bf16[8,2,16,256]{3,2,1,0:T(8,128)(2,1)S(1)}, u32[]{:S(2)}, u32[]{:S(2)}) async-start(bf16[8,2,16,256]{3,2,1,0:T(8,128)(2,1)} %pad_maximum_fusion.2), calls=%async_computation.4 | async-start | bytes 262144 | tf_op jit(solution)/shard_map/all_to_all | solution.py:1005
  226.9 3.0 collective-permute-start.8
  229.8 2.5 all-to-all-done.3
  235.6 2.0 copies_of.2
  237.5 3.6 %all-to-all-start.4 = ((bf16[8,288,256]{2,1,0:T(8,128)(2,1)}), bf16[8,288,256]{2,1,0:T(8,128)(2,1)S(1)}, u32[]{:S(2)}, u32[]{:S(2)}) async-start(bf16[8,288,256]{2,1,0:T(8,128)(2,1)} %copies_of.2), calls=%async_computation.5 | async-start | bytes 2359296 | tf_op jit(solution)/shard_map/all_to_all | solution.py:987
  241.1 11.9 %collective-permute-done.8.rest_1_.two_ref = bf16[1,2,256,1024]{3,2,1,0:T(8,128)(2,1)} collective-permute-done((bf16[1,2,256,1024]{3,2,1,0:T(8,128)(2,1)}, bf16[1,2,256,1024]{3,2,1,0:T(8,128)(2,1)}, u32[]{:S(2)}, u32[]{:S(2)}) %collective-permute-start.8) | collective-permute-done | bytes 1048608 | tf_op jit(solution)/shard_map/ppermute | solution.py:970
  253.0 1.0 copy-done.2
  254.0 1.6 copies_of.3
  255.7 15.0 %all_to_all.31._.mine_ref = bf16[8,128,256]{2,1,0:T(8,128)(2,1)S(1)} all-to-all(bf16[8,128,256]{2,1,0:T(8,128)(2,1)} %copies_of.3), channel_id=1, replica_groups=mesh['zl'=2,'x'=4,'y'=4,'zh'=2,'core'=2] {'y','zh'}, dimensions={0} | all-to-all | bytes 1048576 | tf_op jit(solution)/shard_map/all_to_all | solution.py:987
  270.7 5.8 %collective-permute-start.10 = (bf16[8,128,256]{2,1,0:T(8,128)(2,1)S(1)}, bf16[8,128,256]{2,1,0:T(8,128)(2,1)S(1)}, u32[]{:S(2)}, u32[]{:S(2)}) collective-permute-start(bf16[8,128,256]{2,1,0:T(8,128)(2,1)S(1)} %all_to_all.31._.mine_ref), channel_id=1, source_target_pairs={{0,1},{1,0},{2,3},{3,2},{4,5},{5,4},{6,7},{7,6},{8,9},{9,8},{10,11... | collective-permute-start | bytes 1572872 | tf_op jit(solution)/shard_map/ppermute | solution.py:984
  277.4 3.2 fold.2
  281.2 3.2 fold.3
  286.2 6.6 %update_qkv.1 = (f32[128,3072]{1,0:T(8,128)}, f32[128,3072]{1,0:T(8,128)}, f32[128,3072]{1,0:T(8,128)}, bf16[128,3072]{1,0:T(8,128)(2,1)}) custom-call(s32[1]{0:T(128)} %bitcast.14.core_ref, bf16[8,128,256]{2,1,0:T(8,128)(2,1)} %copy-done.5, bf16[8,128,256]{2,1,0:T(8,128)(2,1)} %copy-done.10, f32[128,3072]{1,0:T(8,128)} %m_ref.6, f32[128,3072]{1,0:T(8,128)} %f_ref.6, ...), custom_call_target="tpu_custom_call" | custom-call | flops 700000000 | bytes 2100000 | tf_op jit(solution)/shard_map/update_qkv/pallas_call | solution.py:818
  293.5 1.1 copy-done.3
  294.5 3.1 update_out.1
  298.2 2.3 finish_out.1
  300.6 7.0 %update_down.1 = (f32[512,1024]{1,0:T(8,128)}, f32[512,1024]{1,0:T(8,128)}, f32[512,1024]{1,0:T(8,128)}, bf16[512,1024]{1,0:T(8,128)(2,1)}) custom-call(s32[1]{0:T(128)} %bitcast.14.core_ref, bf16[8,288,256]{2,1,0:T(8,128)(2,1)} %copy-done.2, bf16[8,288,256]{2,1,0:T(8,128)(2,1)} %copy-done.3, f32[512,1024]{1,0:T(8,128)} %m_ref.7, f32[512,1024]{1,0:T(8,128)} %f_ref.7, ...), custom_call_target="tpu_custom_call" | custom-call | flops 700000000 | bytes 2100000 | tf_op jit(solution)/shard_map/update_down/pallas_call | solution.py:790
  307.6 7.1 %update_up.1 = (f32[128,4096]{1,0:T(8,128)}, f32[128,4096]{1,0:T(8,128)}, f32[128,4096]{1,0:T(8,128)}, bf16[128,4096]{1,0:T(8,128)(2,1)}) custom-call(s32[1]{0:T(128)} %bitcast.14.core_ref, bf16[8,288,256]{2,1,0:T(8,128)(2,1)} %copy-done.2, bf16[8,288,256]{2,1,0:T(8,128)(2,1)} %copy-done.3, f32[128,4096]{1,0:T(8,128)} %m_ref.5, f32[128,4096]{1,0:T(8,128)} %f_ref.5, ...), custom_call_target="tpu_custom_call" | custom-call | flops 700000000 | bytes 2100000 | tf_op jit(solution)/shard_map/update_up/pallas_call | solution.py:737
  315.5 2.9 finish_grad.1
  (100 shorter events, 22.8 us)
Async XLA Ops:
  7.2 3.3 %copy-start = (bf16[128,4096]{1,0:T(8,128)(2,1)S(1)}, bf16[128,4096]{1,0:T(8,128)(2,1)}, u32[]{:S(2)}) copy-start(bf16[128,4096]{1,0:T(8,128)(2,1)} %param.30) | copy-start | bytes 3145732
  7.2 58.3 %all-gather.7.cloned.1.call-start = ((), (), s32[]{:S(2)}) async-start(), calls=%async_computation.9 | async-start | bytes 4718592 | tf_op jit(solution)/shard_map/all_gather | solution.py:949
  7.9 111.0 %all-gather.5.cloned.1.call-start = ((), (), s32[]{:S(2)}) async-start(), calls=%async_computation.8 | async-start | bytes 4718592 | tf_op jit(solution)/shard_map/all_gather | solution.py:950
  24.7 7.8 %copy-start.16 = (s32[1,2048]{1,0:T(1,128)S(1)}, s32[1,2048]{1,0:T(1,128)}, u32[]{:S(2)}) copy-start(s32[1,2048]{1,0:T(1,128)} %param.26) | copy-start | bytes 24580
  24.7 7.8 %copy-start.20 = (s32[1,2048]{1,0:T(1,128)S(1)}, s32[1,2048]{1,0:T(1,128)}, u32[]{:S(2)}) copy-start(s32[1,2048]{1,0:T(1,128)} %param.27) | copy-start | bytes 24580
  24.7 33.0 %all-to-all-start.1 = ((bf16[8,8,16,1024]{3,2,1,0:T(8,128)(2,1)}), bf16[8,8,16,1024]{3,2,1,0:T(8,128)(2,1)S(1)}, u32[]{:S(2)}, u32[]{:S(2)}) async-start(bf16[8,8,16,1024]{3,2,1,0:T(8,128)(2,1)} %broadcast_in_dim.60), calls=%async_computation.1 | async-start | bytes 4194304 | tf_op jit(solution)/shard_map/all_to_all | solution.py:946
  31.2 189.2 %reduce-scatter.2.cloned.1.call-start = ((), (), s32[]{:S(2)}) async-start(), calls=%async_computation.7 | async-start | bytes 5013504 | tf_op jit(solution)/shard_map/reduce_scatter | solution.py:994
  57.7 3.5 %copy-start.4 = (bf16[8,8,16,1024]{3,2,1,0:T(8,128)(2,1)}, bf16[8,8,16,1024]{3,2,1,0:T(8,128)(2,1)S(1)}, u32[]{:S(2)}) copy-start(bf16[8,8,16,1024]{3,2,1,0:T(8,128)(2,1)S(1)} %all-to-all-done.1.w_ref) | copy-start | bytes 6291460
  135.9 30.1 %collective-permute-start.2 = (bf16[1,2,256,1024]{3,2,1,0:T(8,128)(2,1)S(1)}, bf16[1,2,256,1024]{3,2,1,0:T(8,128)(2,1)S(1)}, u32[]{:S(2)}, u32[]{:S(2)}) collective-permute-start(bf16[1,2,256,1024]{3,2,1,0:T(8,128)(2,1)S(1)} %get-tuple-element.111), channel_id=1, source_target_pairs={{0,48},{16,32},{32,16},{48,0},{1,49},{17,33},{33,17},{49,1},{2,50}... | collective-permute-start | bytes 3145736 | tf_op jit(solution)/shard_map/ppermute | solution.py:970
  136.0 30.0 %collective-permute-start = (bf16[1,2,256,1024]{3,2,1,0:T(8,128)(2,1)S(1)}, bf16[1,2,256,1024]{3,2,1,0:T(8,128)(2,1)S(1)}, u32[]{:S(2)}, u32[]{:S(2)}) collective-permute-start(bf16[1,2,256,1024]{3,2,1,0:T(8,128)(2,1)S(1)} %get-tuple-element.112), channel_id=1, source_target_pairs={{0,16},{16,0},{32,48},{48,32},{1,17},{17,1},{33,49},{49,33},{2,18}... | collective-permute-start | bytes 3145736 | tf_op jit(solution)/shard_map/ppermute | solution.py:970
  162.4 26.0 %collective-permute-start.1 = (bf16[1,2,256,1024]{3,2,1,0:T(8,128)(2,1)}, bf16[1,2,256,1024]{3,2,1,0:T(8,128)(2,1)S(1)}, u32[]{:S(2)}, u32[]{:S(2)}) collective-permute-start(bf16[1,2,256,1024]{3,2,1,0:T(8,128)(2,1)} %far_blocks.1), channel_id=1, source_target_pairs={{0,32},{16,48},{32,0},{48,16},{1,33},{17,49},{33,1},{49,17},{2,34}... | collective-permute-start | bytes 3145736 | tf_op jit(solution)/shard_map/ppermute | solution.py:970
  166.0 1.0 copy-start.12
  166.0 1.3 copy-start.13
  182.5 5.9 %collective-permute-start.3 = (f32[8,128,256]{2,1,0:T(8,128)}, f32[8,128,256]{2,1,0:T(8,128)S(1)}, u32[]{:S(2)}, u32[]{:S(2)}) collective-permute-start(f32[8,128,256]{2,1,0:T(8,128)} %get-tuple-element.82), channel_id=1, source_target_pairs={{0,1},{1,0},{2,3},{3,2},{4,5},{5,4},{6,7},{7,6},{8,9},{9,8},{10,11... | collective-permute-start | bytes 3145736 | tf_op jit(solution)/shard_map/ppermute | solution.py:984
  188.4 1.0 copy-start.9
  188.4 1.3 copy-start.11
  193.5 18.1 %all-to-all-start.2 = ((bf16[8,128,256]{2,1,0:T(8,128)(2,1)}), bf16[8,128,256]{2,1,0:T(8,128)(2,1)S(1)}, u32[]{:S(2)}, u32[]{:S(2)}) async-start(bf16[8,128,256]{2,1,0:T(8,128)(2,1)} %pair_sum.1), calls=%async_computation.3 | async-start | bytes 1048576 | tf_op jit(solution)/shard_map/all_to_all | solution.py:987
  203.6 30.0 %collective-permute-start.5 = (bf16[1,2,256,1024]{3,2,1,0:T(8,128)(2,1)}, bf16[1,2,256,1024]{3,2,1,0:T(8,128)(2,1)S(1)}, u32[]{:S(2)}, u32[]{:S(2)}) collective-permute-start(bf16[1,2,256,1024]{3,2,1,0:T(8,128)(2,1)} %get-tuple-element.109), channel_id=1, source_target_pairs={{0,48},{16,32},{32,16},{48,0},{1,49},{17,33},{33,17},{49,1},{2,50}... | collective-permute-start | bytes 3145736 | tf_op jit(solution)/shard_map/ppermute | solution.py:970
  205.2 28.4 %collective-permute-start.4 = (bf16[1,2,256,1024]{3,2,1,0:T(8,128)(2,1)}, bf16[1,2,256,1024]{3,2,1,0:T(8,128)(2,1)S(1)}, u32[]{:S(2)}, u32[]{:S(2)}) collective-permute-start(bf16[1,2,256,1024]{3,2,1,0:T(8,128)(2,1)} %get-tuple-element.110), channel_id=1, source_target_pairs={{0,16},{16,0},{32,48},{48,32},{1,17},{17,1},{33,49},{49,33},{2,18}... | collective-permute-start | bytes 3145736 | tf_op jit(solution)/shard_map/ppermute | solution.py:970
  211.6 0.8 copy-start.15
  222.9 9.4 %all-to-all-start.3 = ((bf16[8,2,16,256]{3,2,1,0:T(8,128)(2,1)}), bf16[8,2,16,256]{3,2,1,0:T(8,128)(2,1)S(1)}, u32[]{:S(2)}, u32[]{:S(2)}) async-start(bf16[8,2,16,256]{3,2,1,0:T(8,128)(2,1)} %pad_maximum_fusion.2), calls=%async_computation.4 | async-start | bytes 262144 | tf_op jit(solution)/shard_map/all_to_all | solution.py:1005
  226.9 26.1 %collective-permute-start.8 = (bf16[1,2,256,1024]{3,2,1,0:T(8,128)(2,1)}, bf16[1,2,256,1024]{3,2,1,0:T(8,128)(2,1)}, u32[]{:S(2)}, u32[]{:S(2)}) collective-permute-start(bf16[1,2,256,1024]{3,2,1,0:T(8,128)(2,1)} %get-tuple-element.108), channel_id=1, source_target_pairs={{0,32},{16,48},{32,0},{48,16},{1,33},{17,49},{33,1},{49,17},{2,34}... | collective-permute-start | bytes 3145736 | tf_op jit(solution)/shard_map/ppermute | solution.py:970
  233.6 1.0 copy-start.7
  234.6 1.0 copy-start.8
  237.5 15.5 %all-to-all-start.4 = ((bf16[8,288,256]{2,1,0:T(8,128)(2,1)}), bf16[8,288,256]{2,1,0:T(8,128)(2,1)S(1)}, u32[]{:S(2)}, u32[]{:S(2)}) async-start(bf16[8,288,256]{2,1,0:T(8,128)(2,1)} %copies_of.2), calls=%async_computation.5 | async-start | bytes 2359296 | tf_op jit(solution)/shard_map/all_to_all | solution.py:987
  253.0 1.0 copy-start.2
  270.7 10.0 %copy-start.5 = (bf16[8,128,256]{2,1,0:T(8,128)(2,1)}, bf16[8,128,256]{2,1,0:T(8,128)(2,1)S(1)}, u32[]{:S(2)}) copy-start(bf16[8,128,256]{2,1,0:T(8,128)(2,1)S(1)} %all_to_all.31._.mine_ref) | copy-start | bytes 1572868
  270.7 14.7 %collective-permute-start.10 = (bf16[8,128,256]{2,1,0:T(8,128)(2,1)S(1)}, bf16[8,128,256]{2,1,0:T(8,128)(2,1)S(1)}, u32[]{:S(2)}, u32[]{:S(2)}) collective-permute-start(bf16[8,128,256]{2,1,0:T(8,128)(2,1)S(1)} %all_to_all.31._.mine_ref), channel_id=1, source_target_pairs={{0,1},{1,0},{2,3},{3,2},{4,5},{5,4},{6,7},{7,6},{8,9},{9,8},{10,11... | collective-permute-start | bytes 1572872 | tf_op jit(solution)/shard_map/ppermute | solution.py:984
  276.5 16.9 %collective-permute-start.7 = (bf16[8,288,256]{2,1,0:T(8,128)(2,1)}, bf16[8,288,256]{2,1,0:T(8,128)(2,1)S(1)}, u32[]{:S(2)}, u32[]{:S(2)}) collective-permute-start(bf16[8,288,256]{2,1,0:T(8,128)(2,1)} %copy-done.2), channel_id=1, source_target_pairs={{0,1},{1,0},{2,3},{3,2},{4,5},{5,4},{6,7},{7,6},{8,9},{9,8},{10,11... | collective-permute-start | bytes 3538952 | tf_op jit(solution)/shard_map/ppermute | solution.py:984
  280.6 4.8 %copy-start.6 = (bf16[8,128,256]{2,1,0:T(8,128)(2,1)S(1)}, bf16[8,128,256]{2,1,0:T(8,128)(2,1)}, u32[]{:S(2)}) copy-start(bf16[8,128,256]{2,1,0:T(8,128)(2,1)} %copy-done.5) | copy-start | bytes 1572868
  280.6 17.0 %collective-permute-start.6 = (bf16[256,1024]{1,0:T(8,128)(2,1)}, bf16[256,1024]{1,0:T(8,128)(2,1)}, u32[]{:S(2)}, u32[]{:S(2)}) collective-permute-start(bf16[256,1024]{1,0:T(8,128)(2,1)} %get-tuple-element.85), channel_id=1, source_target_pairs={{0,64},{64,0},{1,65},{65,1},{2,66},{66,2},{3,67},{67,3},{4,68},{68... | collective-permute-start | bytes 1572872 | tf_op jit(solution)/shard_map/ppermute | solution.py:981
  284.4 30.3 %collective-permute-start.9 = (bf16[256,1024]{1,0:T(8,128)(2,1)}, bf16[256,1024]{1,0:T(8,128)(2,1)S(1)}, u32[]{:S(2)}, u32[]{:S(2)}) collective-permute-start(bf16[256,1024]{1,0:T(8,128)(2,1)} %get-tuple-element.88), channel_id=1, source_target_pairs={{0,64},{64,0},{1,65},{65,1},{2,66},{66,2},{3,67},{67,3},{4,68},{68... | collective-permute-start | bytes 1572872 | tf_op jit(solution)/shard_map/ppermute | solution.py:981
  285.4 0.8 copy-start.10
  286.2 6.6 %copy-start.17 = (f32[128,13]{0,1:T(8,128)S(1)}, f32[128,13]{0,1:T(8,128)}, u32[]{:S(2)}) copy-start(f32[128,13]{0,1:T(8,128)} %param.37) | copy-start | bytes 19972
  286.2 6.6 %copy-start.18 = (f32[128,13]{0,1:T(8,128)S(1)}, f32[128,13]{0,1:T(8,128)}, u32[]{:S(2)}) copy-start(f32[128,13]{0,1:T(8,128)} %param.42) | copy-start | bytes 19972
  286.2 6.6 %copy-start.19 = (f32[128,13]{0,1:T(8,128)S(1)}, f32[128,13]{0,1:T(8,128)}, u32[]{:S(2)}) copy-start(f32[128,13]{0,1:T(8,128)} %param.47) | copy-start | bytes 19972
  293.5 1.1 copy-start.3
  314.7 0.8 copy-start.14
  314.7 3.7 %copy-start.1 = (bf16[128,4096]{1,0:T(8,128)(2,1)S(1)}, bf16[128,4096]{1,0:T(8,128)(2,1)}, u32[]{:S(2)}) copy-start(bf16[128,4096]{1,0:T(8,128)(2,1)} %param.30) | copy-start | bytes 3145732
Sparse Core Ops, SparseCore 0:
  9.7 55.8 all-gather.6
  67.2 51.6 all-gather.4
  134.3 86.0 reduce-scatter.1
